TPU v7x, 256 devices: a whole 4x4x8 slice. The times are simulated.
256 devices in a mesh: seq: 32 (over z, y), ch: 8 (over x, core).
Axes of the slice: x: 4, y: 4, z: 8, core: 2. Of those that a mesh axis runs over, the one named last changes fastest.
Arguments:
- signal: bfloat16 [8192, 4, 768], P('seq', None, 'ch'), may hold values from -6 to 6
- filter_taps: float32 [8192, 768], P('seq', 'ch'), may hold values from -2 to 2
- skip_gain: float32 [768], P('ch'), may hold values from 0.5 to 1.5
- w_gate: bfloat16 [768, 768], P(None, 'ch'), may hold values from -0.21875 to 0.21875
- w_out: bfloat16 [768, 768], P('ch'), may hold values from -0.21875 to 0.21875
- catalogue: bfloat16 [524288, 768], P(('seq', 'ch')), may hold values from -6 to 6
- item_draw_counts: int32 [524288], P(('seq', 'ch')), may hold values from 1 to 8
- sampled_pos: int32 [4096], P('seq'), may hold values from 0 to 1023
- neg_owner: int32 [4096, 64, 1], P('seq'), may hold values from 0 to 255; in each aligned block of 8192 rows (0 to 8191, 8192 to 16383, ..., all dimensions but the last counted through in order) at most 64 rows name the same one
- neg_row: int32 [4096, 64], P('seq'), may hold values from 0 to 2047
- target_owner: int32 [4096, 1], P('seq'), may hold values from 0 to 255; in each aligned block of 128 rows (0 to 127, 128 to 255, ...) at most 2 rows name the same one
- target_row: int32 [4096], P('seq'), may hold values from 0 to 2047
Outputs:
- layer_out: bfloat16 [8192, 4, 768], P('seq', None, 'ch')
- sample_loss: float32 [4096], P('seq')
Inputs may be any that keep to these rules, and one draw needn't show every extreme that they name: `neg_owner`: shard index, devices in seq-major order; of the 8192 samples of one device's positions at most 64 name one shard, a bound that some block reaches. `target_owner`: shard index, devices in seq-major order; of the 128 targets of one device's positions at most 2 name one shard, a bound that some block reaches.
All inputs are finite; a program needn't handle non-finite values.
Results may differ from a plain program's by a relative error of at most 0.007.
Values may be sent and summed in bfloat16 or wider, within the bound.
A program may use at most 128 MiB of HBM per device.

v0:
```python
import math

import jax
import jax.numpy as jnp
from jax import lax
from jax.sharding import PartitionSpec as P

SOFTMAX_TEMP = 0.02
EPSILON = 1e-06
HIGHEST = lax.Precision.HIGHEST


def angle_table(row_count, col_count, period, col_offset):
    left_idx = lax.iota(jnp.int32, row_count)[:, None]
    right_idx = lax.iota(jnp.int32, col_count)[None, :] + col_offset
    phase = left_idx * right_idx % period
    angle = phase.astype(jnp.float32) * (2.0 * math.pi / period)
    return (jnp.cos(angle), jnp.sin(angle))


def first_section(pieces, cos_first, sin_first, cos_twist, sin_twist):
    real_part = jnp.einsum("kn,nrb->krb", cos_first, pieces, precision=HIGHEST)
    imag_part = -jnp.einsum("kn,nrb->krb", sin_first, pieces, precision=HIGHEST)
    return (
        real_part * cos_twist + imag_part * sin_twist,
        imag_part * cos_twist - real_part * sin_twist,
    )


def second_section(real_part, imag_part, cos_full, sin_full):
    out_real = jnp.einsum("kn,jnb->jkb", cos_full, real_part, precision=HIGHEST) + jnp.einsum(
        "kn,jnb->jkb", sin_full, imag_part, precision=HIGHEST
    )
    out_imag = jnp.einsum("kn,jnb->jkb", cos_full, imag_part, precision=HIGHEST) - jnp.einsum(
        "kn,jnb->jkb", sin_full, real_part, precision=HIGHEST
    )
    return (out_real, out_imag)


def inverse_second(real_part, imag_part, cos_full, sin_full):
    out_real = jnp.einsum("nk,jkb->jnb", cos_full, real_part, precision=HIGHEST) - jnp.einsum(
        "nk,jkb->jnb", sin_full, imag_part, precision=HIGHEST
    )
    out_imag = jnp.einsum("nk,jkb->jnb", cos_full, imag_part, precision=HIGHEST) + jnp.einsum(
        "nk,jkb->jnb", sin_full, real_part, precision=HIGHEST
    )
    return (out_real, out_imag)


def make_adder(weight, part_rows):
    return jnp.einsum("tsc,cd->tsd", part_rows, weight, preferred_element_type=jnp.float32)


def slot_ranks(owner_ids, owner_total):
    item_count = owner_ids.shape[0]
    block = math.gcd(item_count, 128)
    block_count = item_count // block
    onehot = (owner_ids[:, None] == lax.iota(jnp.int32, owner_total)[None, :]).astype(jnp.float32)
    onehot = onehot.reshape(block_count, block, owner_total)
    inner_idx = lax.iota(jnp.int32, block)
    lower_inner = (inner_idx[:, None] > inner_idx[None, :]).astype(jnp.float32)
    outer_idx = lax.iota(jnp.int32, block_count)
    lower_outer = (outer_idx[:, None] > outer_idx[None, :]).astype(jnp.float32)
    inside = jnp.einsum("ij,bjk->bik", lower_inner, onehot, precision=HIGHEST)
    earlier = jnp.dot(lower_outer, jnp.sum(onehot, 1), precision=HIGHEST)
    ranks = jnp.sum((inside + earlier[:, None, :]) * onehot, -1)
    return ranks.reshape(item_count).astype(jnp.int32)


def per_device(
    signal,
    filter_taps,
    skip_gain,
    w_gate,
    w_out,
    catalogue,
    item_draw_counts,
    sampled_pos,
    neg_owner,
    neg_row,
    target_owner,
    target_row,
):
    positions, sequences, channels = signal.shape
    groups = lax.axis_size("seq")
    shards = lax.axis_size("ch")
    devices = groups * shards
    own_seq = lax.axis_index("seq")
    piece_len = positions // groups
    period = 2 * groups * positions
    lane_count = sequences * channels
    cos_full, sin_full = angle_table(positions, positions, positions, 0)
    cos_first, sin_first = angle_table(2 * groups, groups, 2 * groups, 0)
    cos_twist, sin_twist = angle_table(2 * groups, piece_len, period, own_seq * piece_len)
    cos_twist = cos_twist[:, :, None]
    sin_twist = sin_twist[:, :, None]
    signal_parts = lax.all_to_all(
        signal.reshape(groups, piece_len, lane_count),
        "seq",
        split_axis=0,
        concat_axis=0,
        tiled=True,
    ).astype(jnp.float32)
    filter_parts = lax.all_to_all(
        filter_taps.reshape(groups, piece_len, channels),
        "seq",
        split_axis=0,
        concat_axis=0,
        tiled=True,
    )
    sig_real, sig_imag = first_section(signal_parts, cos_first, sin_first, cos_twist, sin_twist)
    tap_real, tap_imag = first_section(filter_parts, cos_first, sin_first, cos_twist, sin_twist)
    sig_real, sig_imag, tap_real, tap_imag = (
        lax.all_to_all(sig_real, "seq", split_axis=0, concat_axis=1, tiled=True),
        lax.all_to_all(sig_imag, "seq", split_axis=0, concat_axis=1, tiled=True),
        lax.all_to_all(tap_real, "seq", split_axis=0, concat_axis=1, tiled=True),
        lax.all_to_all(tap_imag, "seq", split_axis=0, concat_axis=1, tiled=True),
    )
    sig_real, sig_imag = second_section(sig_real, sig_imag, cos_full, sin_full)
    tap_real, tap_imag = second_section(tap_real, tap_imag, cos_full, sin_full)
    sig_real = sig_real.reshape(2, positions, sequences, channels)
    sig_imag = sig_imag.reshape(2, positions, sequences, channels)
    tap_real = tap_real[:, :, None, :]
    tap_imag = tap_imag[:, :, None, :]
    prod_real = (sig_real * tap_real - sig_imag * tap_imag).reshape(2, positions, lane_count)
    prod_imag = (sig_real * tap_imag + sig_imag * tap_real).reshape(2, positions, lane_count)
    back_real, back_imag = inverse_second(prod_real, prod_imag, cos_full, sin_full)
    back_real, back_imag = (
        lax.all_to_all(back_real, "seq", split_axis=1, concat_axis=0, tiled=True),
        lax.all_to_all(back_imag, "seq", split_axis=1, concat_axis=0, tiled=True),
    )
    turn_real = back_real * cos_twist - back_imag * sin_twist
    turn_imag = back_imag * cos_twist + back_real * sin_twist
    spatial = (
        jnp.einsum("kn,krb->nrb", cos_first, turn_real, precision=HIGHEST)
        - jnp.einsum("kn,krb->nrb", sin_first, turn_imag, precision=HIGHEST)
    ) / period
    spatial = lax.all_to_all(spatial, "seq", split_axis=0, concat_axis=0, tiled=True)
    convolved = spatial.reshape(positions, sequences, channels)
    gate_sum = make_adder(w_gate, lax.all_gather(signal, "ch", axis=2, tiled=True))
    gated_mix = ((convolved + skip_gain * signal.astype(jnp.float32)) * gate_sum).astype(
        jnp.bfloat16
    )
    partial_terms = jnp.einsum("tsc,cd->tsd", gated_mix, w_out, preferred_element_type=jnp.float32)
    layer_sum = lax.psum_scatter(partial_terms, "ch", scatter_dimension=2, tiled=True)
    layer_out = layer_sum.astype(jnp.bfloat16)
    pos_dev, neg_count = neg_row.shape
    neg_cap = max(2, 2 * pos_dev * neg_count // devices)
    tgt_cap = max(2, 2 * pos_dev // devices)
    slot_total = neg_cap + tgt_cap
    slot_count = devices * slot_total
    neg_owners = neg_owner.reshape(pos_dev * neg_count)
    tgt_owners = target_owner.reshape(pos_dev)
    neg_flat = neg_owners * slot_total + slot_ranks(neg_owners, devices)
    tgt_flat = tgt_owners * slot_total + neg_cap + slot_ranks(tgt_owners, devices)
    request = jnp.zeros((slot_count,), jnp.int32)
    request = (
        request.at[neg_flat].set(neg_row.reshape(pos_dev * neg_count)).at[tgt_flat].set(target_row)
    )
    position_ids = lax.iota(jnp.int32, pos_dev)
    neg_positions = jnp.broadcast_to(position_ids[:, None], (pos_dev, neg_count)).reshape(
        pos_dev * neg_count
    )
    slot_position = (
        jnp.full((slot_count,), -1, jnp.int32)
        .at[neg_flat]
        .set(neg_positions)
        .at[tgt_flat]
        .set(position_ids)
    )
    request = request.reshape(groups, shards, slot_total)
    requested = lax.all_to_all(
        lax.all_to_all(request, "seq", split_axis=0, concat_axis=0, tiled=True),
        "ch",
        split_axis=1,
        concat_axis=1,
        tiled=True,
    )
    column_tables = jnp.moveaxis(catalogue.reshape(catalogue.shape[0], shards, channels), 1, 0)
    wanted = jnp.moveaxis(requested, 1, 0).reshape(shards, groups * slot_total)
    looked_up = jax.vmap(lambda table, rows: jnp.take(table, rows, axis=0))(column_tables, wanted)
    fetched = jnp.moveaxis(looked_up.reshape(shards, groups, slot_total, channels), 0, 1)
    fetched_counts = jnp.take(item_draw_counts, requested, axis=0)
    fetched, fetched_counts = (
        lax.all_to_all(
            lax.all_to_all(fetched, "seq", split_axis=0, concat_axis=0, tiled=True),
            "ch",
            split_axis=1,
            concat_axis=1,
            tiled=True,
        ),
        lax.all_to_all(
            lax.all_to_all(fetched_counts, "seq", split_axis=0, concat_axis=0, tiled=True),
            "ch",
            split_axis=1,
            concat_axis=1,
            tiled=True,
        ),
    )
    fetched = fetched.reshape(slot_count, channels)
    slot_log = jnp.log(fetched_counts.reshape(slot_count).astype(jnp.float32))
    token_rows = positions * sequences
    pick = (sampled_pos[:, None] == lax.iota(jnp.int32, token_rows)[None, :]).astype(jnp.bfloat16)
    queries = jnp.dot(
        pick, layer_out.reshape(token_rows, channels), preferred_element_type=jnp.float32
    ).astype(jnp.bfloat16)
    query_f = queries.astype(jnp.float32)
    fetched_f = fetched.astype(jnp.float32)
    slot_mask = slot_position[:, None] == position_ids[None, :]
    all_products = lax.dot_general(
        fetched, queries, (((1,), (1,)), ((), ())), preferred_element_type=jnp.float32
    )
    slot_products = jnp.sum(jnp.where(slot_mask, all_products, 0.0), 1)
    slot_square = jnp.sum(fetched_f * fetched_f, -1)
    query_square = jnp.sum(query_f * query_f, -1)
    slot_products, slot_square, query_square = (
        lax.psum(slot_products.astype(jnp.bfloat16), "ch").astype(jnp.float32),
        lax.psum(slot_square.astype(jnp.bfloat16), "ch").astype(jnp.float32),
        lax.psum(query_square.astype(jnp.bfloat16), "ch").astype(jnp.float32),
    )
    total_width = channels * shards
    query_norm_scale = lax.rsqrt(query_square / total_width + EPSILON)
    slot_query_scale = jnp.sum(jnp.where(slot_mask, query_norm_scale[None, :], 0.0), 1)
    slot_logit = (
        slot_products
        * slot_query_scale
        * lax.rsqrt(slot_square / total_width + EPSILON)
        / (total_width * SOFTMAX_TEMP)
        - slot_log
    )
    is_target = lax.iota(jnp.int32, slot_count) % slot_total >= neg_cap
    target_mask = slot_mask & is_target[:, None]
    negative_mask = slot_mask & jnp.logical_not(is_target)[:, None]
    target_logit = jnp.sum(jnp.where(target_mask, slot_logit[:, None], 0.0), 0)
    slot_exp = jnp.exp(jnp.where(slot_position >= 0, slot_logit, 0.0))
    negative_total = jnp.sum(jnp.where(negative_mask, slot_exp[:, None], 0.0), 0)
    sample_loss = jnp.log(jnp.exp(target_logit) + negative_total) - target_logit
    return (layer_out, sample_loss)


def solution(mesh):
    placed = (
        P("seq", None, "ch"),
        P("seq", "ch"),
        P("ch"),
        P(None, "ch"),
        P("ch", None),
        P(("seq", "ch"), None),
        P(("seq", "ch")),
        P("seq"),
        P("seq", None, None),
        P("seq", None),
        P("seq", None),
        P("seq"),
    )
    return jax.shard_map(
        per_device,
        mesh=mesh,
        in_specs=placed,
        out_specs=(P("seq", None, "ch"), P("seq")),
        check_vma=False,
    )
```

profile of v0, /device:TPU:1, one launch (start us, length us, event | category | flops | bytes accessed | tf_op | source)
XLA Modules:
  0.0 1268.3 jit_solution(13098215904689541242)
XLA Ops:
  17.4 30.5 %scatter_custom_fusion.2 = s32[16896]{0:T(1024)S(1)} fusion(s32[8192]{0:T(1024)S(1)} %bitcast.201, s32[8192]{0:T(1024)S(1)} %reshape.364, s32[]{:T(128)} %constant.72.clone.1), kind=kCustom, calls=%fused_computation.156 | custom fusion | bytes 67588 | tf_op jit(solution)/shard_map/scatter | solution.py:158
  49.7 12.0 all-to-all-start.9
  63.5 7.5 all-to-all-done.9
  75.0 9.3 all-to-all-done.3
  90.1 8.1 all-to-all-done
  102.9 9.7 all-to-all-done.4
  119.3 7.8 all-to-all-done.5
  132.3 14.1 %all-to-all-done.1 = f32[64,8,384]{2,1,0:T(8,128)S(1)} async-done(((f32[64,8,384]{2,1,0:T(8,128)}), f32[64,8,384]{2,1,0:T(8,128)S(1)}, u32[]{:S(2)}, u32[]{:S(2)}) %all-to-all-start.1) | async-done | bytes 786464 | tf_op jit(solution)/shard_map/all_to_all | solution.py:114
  146.4 7.2 all-to-all-start.2
  163.5 5.4 all-to-all-done.2
  168.9 13.8 %all-to-all-start.10 = ((s32[32,8,66]{2,0,1:T(8,128)}), s32[32,8,66]{2,0,1:T(8,128)S(1)}, u32[]{:S(2)}, u32[]{:S(2)}) async-start(s32[32,8,66]{2,0,1:T(8,128)} %copy.159), calls=%async_computation.11 | async-start | bytes 262144 | tf_op jit(solution)/shard_map/all_to_all | solution.py:172
  204.4 17.4 %all-to-all-done.6 = f32[2,256,384]{2,0,1:T(2,128)S(1)} async-done(((f32[2,256,384]{2,0,1:T(2,128)}), f32[2,256,384]{2,0,1:T(2,128)S(1)}, u32[]{:S(2)}, u32[]{:S(2)}) %all-to-all-start.6) | async-done | bytes 786464 | tf_op jit(solution)/shard_map/all_to_all | solution.py:129
  222.7 5.2 all-to-all-start.7
  237.6 10.8 all-to-all-done.7
  253.1 6.4 all-to-all-start.8
  259.6 300.7 %gather_fusion.1 = bf16[16896,96]{1,0:T(8,128)(2,1)} fusion(bf16[8,2048,96]{2,1,0:T(8,128)(2,1)} %bitcast.186, s32[16896]{0:T(1024)S(1)} %reshape.338), kind=kCustom, calls=%fused_computation.1 | custom fusion | bytes 6623232 | tf_op jit(solution)/shard_map/vmap(jit(_take))/gather | solution.py:181
  560.3 7.1 gather.11
  567.5 8.2 select_bitcast_fusion
  575.7 7.0 copy.162
  582.8 378.8 %all-to-all-start.11 = ((bf16[32,8,66,96]{3,1,2,0:T(8,128)(2,1)}), bf16[32,8,66,96]{3,1,2,0:T(8,128)(2,1)}, u32[]{:S(2)}, u32[]{:S(2)}) async-start(bf16[32,8,66,96]{3,1,2,0:T(8,128)(2,1)} %copy.162), calls=%async_computation.12 | async-start | bytes 8650752 | tf_op jit(solution)/shard_map/all_to_all | solution.py:186
  962.9 35.9 %all-gather.2.cloned.1.call-done = bf16[256,4,768]{0,2,1:T(8,128)(2,1)} async-done(((bf16[256,4,96]{0,2,1:T(8,128)(2,1)}), bf16[256,4,768]{0,2,1:T(8,128)(2,1)}) %all-gather.2.cloned.1.call-update) | async-done | bytes 1572880 | tf_op jit(solution)/shard_map/all_gather | solution.py:140
  1003.0 86.9 %gather_fusion = s32[16896]{0:T(1024)S(1)} fusion(s32[2048]{0:T(1024)S(1)} %copy-done.2, s32[17408]{0:T(1024)S(1)} %pad_clamp_fusion), kind=kCustom, calls=%fused_computation | custom fusion | bytes 202752 | tf_op jit(solution)/shard_map/jit(_take)/gather | solution.py:183
  1090.8 9.6 all-to-all-start.13
  1100.4 5.3 copy.163
  1109.9 6.7 all-to-all-start.12
  1116.6 30.5 %scatter_custom_fusion = s32[16896]{0:T(1024)S(1)} fusion(s32[8192]{0:T(1024)S(1)} %bitcast.202, s32[8192]{0:T(1024)S(1)} %reshape.348, s32[]{:T(128)} %constant.117.clone.1), kind=kCustom, calls=%fused_computation.158 | custom fusion | bytes 67588 | tf_op jit(solution)/shard_map/scatter | solution.py:167
  1148.9 17.9 %all-to-all-done.12 = bf16[32,8,66,96]{3,0,2,1:T(8,128)(2,1)} async-done(((bf16[32,8,66,96]{3,0,2,1:T(8,128)(2,1)}), bf16[32,8,66,96]{3,0,2,1:T(8,128)(2,1)}, u32[]{:S(2)}, u32[]{:S(2)}) %all-to-all-start.12) | async-done | bytes 3244064 | tf_op jit(solution)/shard_map/all_to_all | solution.py:185
  1170.9 4.6 multiply_reduce_fusion
  1176.4 6.1 copy.164
  1182.6 7.4 reshape.328
  1196.6 55.3 %all-reduce.3.cloned.1.call-done = (bf16[16896]{0:T(1024)(128)(2,1)}, bf16[128]{0:T(256)(128)(2,1)}, bf16[16896]{0:T(1024)(128)(2,1)}) async-done(((bf16[16896]{0:T(1024)(128)(2,1)}, bf16[128]{0:T(256)(128)(2,1)}, bf16[16896]{0:T(1024)(128)(2,1)}), (bf16[16896]{0:T(1024)(128)(2,1)}, bf16[128]{0:T(256)(128)(2,1)}, bf16[16896]{0:T(1024)(128)(2,1)})) %all-reduce.3.cloned.1.call-update) | async-done | bytes 67856 | tf_op jit(solution)/shard_map/psum | solution.py:218
  1254.7 6.1 select_reduce_fusion
  (132 shorter events, 114.3 us)
Async XLA Ops:
  7.2 991.6 %copy-start = (bf16[96,768]{1,0:T(8,128)(2,1)S(1)}, bf16[96,768]{1,0:T(8,128)(2,1)}, u32[]{:S(2)}) copy-start(bf16[96,768]{1,0:T(8,128)(2,1)} %param.16) | copy-start | bytes 442372
  14.1 33.7 %copy-start.9 = (s32[128]{0:T(128)S(1)}, s32[128]{0:T(128)}, u32[]{:S(2)}) copy-start(s32[128]{0:T(128)} %param.23) | copy-start | bytes 1540
  14.1 47.6 %copy-start.8 = (f32[256,96]{0,1:T(8,128)S(1)}, f32[256,96]{0,1:T(8,128)}, u32[]{:S(2)}) copy-start(f32[256,96]{0,1:T(8,128)} %param.13) | copy-start | bytes 294916
  14.1 48.4 %copy-start.4 = (bf16[256,4,96]{0,2,1:T(8,128)(2,1)S(1)}, bf16[256,4,96]{0,2,1:T(8,128)(2,1)}, u32[]{:S(2)}) copy-start(bf16[256,4,96]{0,2,1:T(8,128)(2,1)} %param.12) | copy-start | bytes 589828
  49.7 21.4 %all-to-all-start.9 = ((s32[32,8,66]{2,1,0:T(8,128)}), s32[32,8,66]{2,1,0:T(8,128)S(1)}, u32[]{:S(2)}, u32[]{:S(2)}) async-start(s32[32,8,66]{2,1,0:T(8,128)} %reshape.325), calls=%async_computation.10 | async-start | bytes 262144 | tf_op jit(solution)/shard_map/all_to_all | solution.py:173
  71.1 13.3 %all-to-all-start.3 = ((f32[32,8,96]{2,1,0:T(8,128)}), f32[32,8,96]{2,1,0:T(8,128)S(1)}, u32[]{:S(2)}, u32[]{:S(2)}) async-start(f32[32,8,96]{2,1,0:T(8,128)} %bitcast.11), calls=%async_computation.3 | async-start | bytes 262144 | tf_op jit(solution)/shard_map/all_to_all | solution.py:104
  84.3 13.9 %all-to-all-start = ((bf16[32,8,384]{2,1,0:T(8,128)(2,1)}), bf16[32,8,384]{2,1,0:T(8,128)(2,1)S(1)}, u32[]{:S(2)}, u32[]{:S(2)}) async-start(bf16[32,8,384]{2,1,0:T(8,128)(2,1)} %reshape.320), calls=%async_computation | async-start | bytes 393216 | tf_op jit(solution)/shard_map/all_to_all | solution.py:97
  98.2 14.4 %all-to-all-start.4 = ((f32[64,8,96]{2,1,0:T(8,128)}), f32[64,8,96]{2,1,0:T(8,128)S(1)}, u32[]{:S(2)}, u32[]{:S(2)}) async-start(f32[64,8,96]{2,1,0:T(8,128)} %copy.138), calls=%async_computation.4 | async-start | bytes 524288 | tf_op jit(solution)/shard_map/all_to_all | solution.py:116
  112.6 14.5 %all-to-all-start.5 = ((f32[64,8,96]{2,1,0:T(8,128)}), f32[64,8,96]{2,1,0:T(8,128)S(1)}, u32[]{:S(2)}, u32[]{:S(2)}) async-start(f32[64,8,96]{2,1,0:T(8,128)} %copy.141), calls=%async_computation.5 | async-start | bytes 524288 | tf_op jit(solution)/shard_map/all_to_all | solution.py:117
  127.1 19.3 %all-to-all-start.1 = ((f32[64,8,384]{2,1,0:T(8,128)}), f32[64,8,384]{2,1,0:T(8,128)S(1)}, u32[]{:S(2)}, u32[]{:S(2)}) async-start(f32[64,8,384]{2,1,0:T(8,128)} %copy.129), calls=%async_computation.1 | async-start | bytes 1572864 | tf_op jit(solution)/shard_map/all_to_all | solution.py:114
  146.4 22.5 %all-to-all-start.2 = ((f32[64,8,384]{2,1,0:T(8,128)}), f32[64,8,384]{2,1,0:T(8,128)S(1)}, u32[]{:S(2)}, u32[]{:S(2)}) async-start(f32[64,8,384]{2,1,0:T(8,128)} %copy.132), calls=%async_computation.2 | async-start | bytes 1572864 | tf_op jit(solution)/shard_map/all_to_all | solution.py:115
  168.9 26.2 %all-to-all-start.10 = ((s32[32,8,66]{2,0,1:T(8,128)}), s32[32,8,66]{2,0,1:T(8,128)S(1)}, u32[]{:S(2)}, u32[]{:S(2)}) async-start(s32[32,8,66]{2,0,1:T(8,128)} %copy.159), calls=%async_computation.11 | async-start | bytes 262144 | tf_op jit(solution)/shard_map/all_to_all | solution.py:172
  195.1 26.7 %all-to-all-start.6 = ((f32[2,256,384]{2,0,1:T(2,128)}), f32[2,256,384]{2,0,1:T(2,128)S(1)}, u32[]{:S(2)}, u32[]{:S(2)}) async-start(f32[2,256,384]{2,0,1:T(2,128)} %copy.148), calls=%async_computation.6 | async-start | bytes 1572864 | tf_op jit(solution)/shard_map/all_to_all | solution.py:129
  221.8 0.9 copy-start.3
  222.7 25.7 %all-to-all-start.7 = ((f32[2,256,384]{2,0,1:T(2,128)}), f32[2,256,384]{2,0,1:T(2,128)}, u32[]{:S(2)}, u32[]{:S(2)}) async-start(f32[2,256,384]{2,0,1:T(2,128)} %copy.151), calls=%async_computation.7 | async-start | bytes 1572864 | tf_op jit(solution)/shard_map/all_to_all | solution.py:130
  253.1 329.7 %all-to-all-start.8 = ((f32[32,8,384]{2,1,0:T(8,128)}), f32[32,8,384]{2,1,0:T(8,128)S(1)}, u32[]{:S(2)}, u32[]{:S(2)}) async-start(f32[32,8,384]{2,1,0:T(8,128)} %copy.154), calls=%async_computation.8 | async-start | bytes 786432 | tf_op jit(solution)/shard_map/all_to_all | solution.py:138
  582.7 416.0 %copy-start.5 = (bf16[256,4,96]{0,2,1:T(8,128)(2,1)S(1)}, bf16[256,4,96]{0,2,1:T(8,128)(2,1)}, u32[]{:S(2)}) copy-start(bf16[256,4,96]{0,2,1:T(8,128)(2,1)} %param.12) | copy-start | bytes 589828
  582.8 416.0 %copy-start.7 = (bf16[768,96]{0,1:T(8,128)(2,1)S(1)}, bf16[768,96]{0,1:T(8,128)(2,1)}, u32[]{:S(2)}) copy-start(bf16[768,96]{0,1:T(8,128)(2,1)} %param.15) | copy-start | bytes 442372
  582.8 416.0 %copy-start.10 = (f32[96]{0:T(128)S(1)}, f32[96]{0:T(128)}, u32[]{:S(2)}) copy-start(f32[96]{0:T(128)} %param.14) | copy-start | bytes 1156
  582.8 508.1 %all-to-all-start.11 = ((bf16[32,8,66,96]{3,1,2,0:T(8,128)(2,1)}), bf16[32,8,66,96]{3,1,2,0:T(8,128)(2,1)}, u32[]{:S(2)}, u32[]{:S(2)}) async-start(bf16[32,8,66,96]{3,1,2,0:T(8,128)(2,1)} %copy.162), calls=%async_computation.12 | async-start | bytes 8650752 | tf_op jit(solution)/shard_map/all_to_all | solution.py:186
  961.5 37.2 %all-gather.2.cloned.1.call-start = ((), (), s32[]{:S(2)}) async-start(), calls=%async_computation.16 | async-start | bytes 1769472 | tf_op jit(solution)/shard_map/all_gather | solution.py:140
  962.3 227.7 %reduce-scatter.2.cloned.1.call-start = ((), (), s32[]{:S(2)}) async-start(), calls=%async_computation.17 | async-start | bytes 3538944 | tf_op jit(solution)/shard_map/reduce_scatter | solution.py:145
  962.9 40.1 %copy-start.2 = (s32[2048]{0:T(1024)S(1)}, s32[2048]{0:T(1024)}, u32[]{:S(2)}) copy-start(s32[2048]{0:T(1024)} %param.18) | copy-start | bytes 24580
  1090.8 19.0 %all-to-all-start.13 = ((s32[32,8,66]{2,1,0:T(8,128)}), s32[32,8,66]{2,1,0:T(8,128)S(1)}, u32[]{:S(2)}, u32[]{:S(2)}) async-start(s32[32,8,66]{2,1,0:T(8,128)} %and_select_fusion), calls=%async_computation.14 | async-start | bytes 262144 | tf_op jit(solution)/shard_map/all_to_all | solution.py:193
  1109.9 56.9 %all-to-all-start.12 = ((bf16[32,8,66,96]{3,0,2,1:T(8,128)(2,1)}), bf16[32,8,66,96]{3,0,2,1:T(8,128)(2,1)}, u32[]{:S(2)}, u32[]{:S(2)}) async-start(bf16[32,8,66,96]{3,0,2,1:T(8,128)(2,1)} %copy.163), calls=%async_computation.13 | async-start | bytes 8650752 | tf_op jit(solution)/shard_map/all_to_all | solution.py:185
  1166.8 29.5 %all-to-all-start.14 = ((s32[32,8,66]{2,0,1:T(8,128)}), s32[32,8,66]{2,0,1:T(8,128)S(1)}, u32[]{:S(2)}, u32[]{:S(2)}) async-start(s32[32,8,66]{2,0,1:T(8,128)} %copy.171), calls=%async_computation.15 | async-start | bytes 262144 | tf_op jit(solution)/shard_map/all_to_all | solution.py:192
  1170.9 80.9 %all-reduce.3.cloned.1.call-start = ((), (), s32[]{:S(2)}) async-start(), calls=%async_computation.18 | async-start | bytes 140288 | tf_op jit(solution)/shard_map/psum | solution.py:218
  1182.6 8.6 copy-start.11
  1191.0 5.3 copy-start.6
  1192.0 69.3 %copy-start.1 = (bf16[96,768]{1,0:T(8,128)(2,1)S(1)}, bf16[96,768]{1,0:T(8,128)(2,1)}, u32[]{:S(2)}) copy-start(bf16[96,768]{1,0:T(8,128)(2,1)} %param.16) | copy-start | bytes 442372
Sparse Core Ops, SparseCore 0:
  964.2 34.4 all-gather.1
  1002.9 36.3 reduce-scatter.1
  1196.4 55.4 all-reduce.2
where the time goes:
time: 1280 us; the launch traced here: 1270 us
  local copies, waits for them, and re-layouts  513 us (40%)
  starting transfers between devices  468 us (37%)
  waiting for transfers between devices  204 us (16%)
  matrix products  41.1 us (3%)
  other arithmetic  28 us (2%)
  between operations  14.8 us (1%)
    all_to_all x1, starting transfers between devices, per_device(): lax.all_to_all(fetched, 'seq', split_axis=0, concat_axis=0, tiled=True)  379 us
    gather x3, local copies, waits for them, and re-layouts, per_device(): jnp.take(table, rows, axis=0)  308 us
    gather x2, local copies, waits for them, and re-layouts, per_device(): fetched_counts = jnp.take(item_draw_counts, requested, axis=0)  87 us
    psum x1, waiting for transfers between devices, per_device(): lax.psum(slot_square.astype(jnp.bfloat16), 'ch').astype(jnp.float32)  55.3 us
    all_gather x1, waiting for transfers between devices, per_device(): lax.all_gather(signal, 'ch', axis=2, tiled=True)  35.9 us
    scatter x2, local copies, waits for them, and re-layouts, per_device(): request.at[neg_flat].set(neg_row.reshape(pos_dev * neg_count)).at[tgt_flat]  31.5 us
    scatter x2, local copies, waits for them, and re-layouts, per_device(): slot_position = jnp.full((slot_count,), -1, jnp.int32).at[neg_flat].set(n...  31.5 us
  transfers between devices with their start and end apart: 18, of which 13 were waited for; matrix products, arithmetic and copies ran while one was open for 41% of the time, Pallas kernels for 0%

commit v1 on v0

v1 whole, which is shorter than its diff:
```python
import jax
import jax.numpy as jnp
from jax import lax
from jax.experimental import pallas as pl
from jax.experimental.pallas import tpu as pltpu
from jax.sharding import PartitionSpec as P

SOFTMAX_TEMP = 0.02
EPSILON = 1e-06
MESH = pl.DeviceIdType.MESH
BF16 = jnp.bfloat16
F32 = jnp.float32
I32 = jnp.int32

S = 32
C = 8
LANE = 128
CH = 96
FULL = CH * C
TOK = 1024
NEG = 64
GROUPS = 16
SLOTS = (GROUPS + 1) * LANE
ITEMS = 2048

(
    X_CONV,
    X_REQ,
    X_BACK,
    X_QUERY,
    X_SUMS,
    X_SIG,
    X_WGATE,
    X_WOUT,
    X_TABLE,
    X_ROWS,
    X_MIX,
    X_OUT,
    X_PART,
    X_FIN,
) = range(14)


def iota(shape, dim):
    return lax.broadcasted_iota(I32, shape, dim)


def onehot(mask):
    return jnp.where(mask, 1.0, 0.0).astype(BF16)


def dot(a, b, ca=1, cb=0):
    return lax.dot_general(a, b, (((ca,), (cb,)), ((), ())), preferred_element_type=F32)


def split_parts(value, count):
    parts = []
    for _ in range(count):
        piece = value.astype(BF16)
        parts.append(piece)
        value = value - piece.astype(F32)
    return parts


def body(
    sig,
    taps,
    gain,
    w_gate,
    w_out,
    cat,
    cnt,
    spos,
    nown,
    nrow,
    town,
    trow,
    out_ref,
    loss_ref,
    perm,
    sig_send,
    sig_all,
    msgf,
    msg1,
    rcv1,
    rf,
    xpad,
    x4,
    acc,
    msg2,
    rcv2,
    wg_own,
    wg_all,
    wo_all,
    wo_t,
    gate_t,
    mix_send,
    mix_all,
    lo_send,
    lo_all,
    q_own,
    q_all,
    req_msg,
    req_all,
    ohs,
    inner,
    total,
    keys,
    vals,
    tab_own,
    tab_all,
    cat_t,
    rows_send,
    rows_all,
    row_scale,
    row_log,
    ohp,
    oht,
    part,
    part_all,
    sums,
    sums_all,
    fin,
    fin_all,
    send_sem,
    recv_sem,
):
    me_s = lax.axis_index("seq")
    me_c = lax.axis_index("ch")

    def seq_copy(x, peer, src, dst):
        return pltpu.make_async_remote_copy(
            src_ref=src,
            dst_ref=dst,
            send_sem=send_sem.at[x, peer],
            recv_sem=recv_sem.at[x, me_s],
            device_id=(peer, me_c),
            device_id_type=MESH,
        )

    def ch_copy(x, peer, src, dst):
        return pltpu.make_async_remote_copy(
            src_ref=src,
            dst_ref=dst,
            send_sem=send_sem.at[x, peer],
            recv_sem=recv_sem.at[x, me_c],
            device_id=(me_s, peer),
            device_id_type=MESH,
        )

    def over(n, me, fn):
        def step(d, carry):
            fn(lax.rem(me + d, n))
            return carry

        lax.fori_loop(1, n, step, 0)

    def start_seq(x, src_of, dst):
        over(S, me_s, lambda peer: seq_copy(x, peer, src_of(peer), dst.at[me_s]).start())

    def start_ch(x, src_of, dst):
        over(C, me_c, lambda peer: ch_copy(x, peer, src_of(peer), dst.at[me_c]).start())

    def wait_from(x, peer, src, dst, device):
        pltpu.make_async_remote_copy(
            src_ref=src,
            dst_ref=dst,
            send_sem=send_sem.at[x, peer],
            recv_sem=recv_sem.at[x, peer],
            device_id=device,
            device_id_type=MESH,
        ).wait_recv()

    def wait_seq(x, src_of, dst):
        over(S, me_s, lambda peer: wait_from(x, peer, src_of(peer), dst.at[peer], (peer, me_c)))

    def wait_ch(x, src_of, dst):
        over(C, me_c, lambda peer: wait_from(x, peer, src_of(peer), dst.at[peer], (me_s, peer)))

    def sent_seq(x, src_of, dst):
        over(S, me_s, lambda peer: seq_copy(x, peer, src_of(peer), dst.at[me_s]).wait_send())

    def sent_ch(x, src_of, dst):
        over(C, me_c, lambda peer: ch_copy(x, peer, src_of(peer), dst.at[me_c]).wait_send())

    barrier = pltpu.get_barrier_semaphore()

    def greet_seq(peer):
        pl.semaphore_signal(barrier, inc=1, device_id=(peer, me_c), device_id_type=MESH)

    def greet_ch(peer):
        pl.semaphore_signal(barrier, inc=1, device_id=(me_s, peer), device_id_type=MESH)

    over(S, me_s, greet_seq)
    over(C, me_c, greet_ch)

    col = iota((TOK, TOK), 1)
    token = ((col >> 9) * LANE + (col & 127)) * 4 + ((col >> 7) & 3)
    perm[...] = onehot(iota((TOK, TOK), 0) == token)
    sig_t = dot(sig[...], perm[...], 0, 0)
    eye = onehot(iota((256, 256), 0) == iota((256, 256), 1))
    taps_t = dot(taps[...].astype(BF16), eye, 0, 0)
    msgf[...] = jnp.zeros_like(msgf)
    for q in range(8):
        piece = sig_t[:, q * LANE : (q + 1) * LANE]
        sig_send[q] = piece.astype(BF16)
        for k in range(3):
            msgf[pl.ds(k * 8 + q, S, stride=32), :] = piece[k * 32 : (k + 1) * 32]
    for il in range(2):
        piece = taps_t[:, il * LANE : (il + 1) * LANE]
        for k in range(3):
            msgf[pl.ds(24 + 2 * k + il, S, stride=32), :] = piece[k * 32 : (k + 1) * 32]
    msg1[...] = msgf[...].reshape(S, 32, LANE).astype(BF16)

    pl.semaphore_wait(barrier, S - 1 + C - 1)

    start_seq(X_CONV, lambda p: msg1.at[p], rcv1)
    rcv1[me_s] = msg1[me_s]
    start_ch(X_SIG, lambda p: sig_send.at[p], sig_all)
    sig_all[me_c] = sig_send[me_c]
    wg_own[...] = w_gate[...].astype(F32).T.astype(BF16)
    start_ch(X_WGATE, lambda p: wg_own, wg_all)
    wg_all[me_c] = wg_own[...]
    start_ch(X_WOUT, lambda p: w_out, wo_all)
    wo_all[me_c] = w_out[...]

    upper = onehot(iota((LANE, LANE), 0) < iota((LANE, LANE), 1))
    ones = jnp.ones((LANE, LANE), BF16)
    owner_ids = iota((S, LANE), 0)

    def own_onehot(owners):
        mine = jnp.where((owners & 7) == me_c, owners >> 3, -1)
        return jnp.where(owner_ids == mine, 1.0, 0.0)

    def mark(m, carry):
        ohs[pl.ds(pl.multiple_of(m * S, S), S), :] = own_onehot(nown[pl.ds(m, 1), :]).astype(BF16)
        return carry

    lax.fori_loop(0, 64, mark, 0)
    inner[...] = dot(ohs[...], upper)
    total[...] = dot(ohs[...], ones)
    key_ids = iota((LANE, LANE), 0).astype(F32)
    lane_row = iota((1, LANE), 1)

    def key_of(hot, rank, offset):
        found = jnp.sum(hot * (rank + 1.0), axis=0, keepdims=True)
        place = jnp.where(found > 0.5, found - 1.0 + offset, -1.0)
        return jnp.where(key_ids == place, 1.0, 0.0).astype(BF16)

    def value_of(hot, rows, pos):
        high = (rows >> 8).astype(F32)
        low = (rows & 255).astype(F32)
        pieces = [hot * high, hot * low, hot * pos.astype(F32), hot]
        return jnp.concatenate(pieces, axis=0).astype(BF16)

    neg_offset = (lax.rem(me_s, 2) * NEG).astype(F32)

    def place(m, before):
        rows = pl.ds(pl.multiple_of(m * S, S), S)
        lanes = pl.ds(pl.multiple_of(m * LANE, LANE), LANE)
        hot = ohs[rows, :].astype(F32)
        keys[:, lanes] = key_of(hot, inner[rows, :] + before, neg_offset)
        vals[:, lanes] = value_of(hot, nrow[pl.ds(m, 1), :], 2 * m + (lane_row >> 6))
        return before + total[rows, :]

    lax.fori_loop(0, 64, place, jnp.zeros((S, LANE), F32))

    def packed(found):
        high, low, pos, filled = (found[i * S : (i + 1) * S].astype(I32) for i in range(4))
        return jnp.where(filled > 0, (high * 256 + low) * LANE + pos, -1)

    neg_table = packed(dot(vals[...], keys[...], 1, 1))
    hot = own_onehot(town[...])
    rank = dot(hot.astype(BF16), upper)
    tgt_table = packed(
        dot(
            value_of(hot, trow[...], lane_row),
            key_of(hot, rank, (2 * me_s).astype(F32)),
            1,
            1,
        )
    )
    req_msg[...] = jnp.full(req_msg.shape, -1, I32)
    req_msg[:, 0, :] = neg_table
    req_msg[:, 1, :] = tgt_table
    start_seq(X_REQ, lambda p: req_msg.at[p], req_all)
    req_all[me_s] = req_msg[me_s]

    def turn(i, carry):
        span = pl.ds(pl.multiple_of(i * 256, 256), 256)
        cat_t[0:FULL, span] = cat[span, :].T
        return carry

    lax.fori_loop(0, ITEMS // 256, turn, 0)
    cat_t[FULL : FULL + 16, :] = jnp.broadcast_to(cnt[...].astype(F32), (16, ITEMS)).astype(BF16)

    wait_seq(X_CONV, lambda p: msg1.at[p], rcv1)
    rf[...] = rcv1[...].astype(F32)
    xpad[0:16, :] = jnp.zeros((16, LANE), F32)
    later = iota((LANE, LANE), 1) >= iota((LANE, LANE), 0)
    msgf[...] = jnp.zeros_like(msgf)

    for k in range(3):
        xpad[16:272, :] = rf[:, k * 8 : (k + 1) * 8, :].reshape(256, LANE)
        x4[...] = jnp.concatenate(
            [xpad[16 - 4 * j : 272 - 4 * j, :] for j in range(4)], axis=1
        ).astype(BF16)
        acc[...] = jnp.zeros_like(acc)
        prev = jnp.zeros((LANE, LANE), F32)
        for e in range(16):
            tiles = []
            for j in range(4):
                d = 4 * e + j
                row = 24 + 2 * k + d % 2
                chunk = jnp.broadcast_to(rf[d // 2, row : row + 1, :], (LANE, LANE))
                turned = pltpu.roll(chunk, 0, 1, stride=1, stride_axis=0)
                tiles.append(jnp.where(later, turned, prev).astype(BF16))
                prev = turned
            taps_tile = jnp.concatenate(tiles, axis=0)
            acc[16 * e :, :] += dot(x4[0 : 256 - 16 * e, :], taps_tile)
        for s in range(S):
            msgf[s * 32 + k * 8 : s * 32 + k * 8 + 8, :] = acc[s * 8 : s * 8 + 8, :]
    msg2[...] = msgf[...].reshape(S, 32, LANE).astype(BF16)
    start_seq(X_BACK, lambda p: msg2.at[p], rcv2)
    rcv2[me_s] = msg2[me_s]

    wait_seq(X_REQ, lambda p: req_msg.at[p], req_all)
    asked = req_all[...]
    asked_neg = asked[:, 0, :].reshape(GROUPS, 2, LANE)
    lane16 = iota((GROUPS, LANE), 1)
    tab_own[...] = jnp.full(tab_own.shape, -1, I32)
    tab_own[0:GROUPS, :] = jnp.where(lane16 < NEG, asked_neg[:, 0, :], asked_neg[:, 1, :])
    tab_own[GROUPS : GROUPS + 1, :] = jnp.max(asked[:, 1, :], axis=0, keepdims=True)
    start_ch(X_TABLE, lambda p: tab_own, tab_all)
    tab_all[me_c] = tab_own[...]
    row_scale[...] = jnp.zeros_like(row_scale)
    row_log[...] = jnp.zeros_like(row_log)
    item_ids = iota((ITEMS, LANE), 0)

    def picked(group):
        return onehot(item_ids == (tab_own[pl.ds(group, 1), :] >> 7))

    def keep(found, lane0, width, group0):
        for c in range(C):
            rows_send[c, :, pl.ds(lane0, width)] = found[c * CH : (c + 1) * CH].astype(BF16)
        square = jnp.sum(found[0:FULL] * found[0:FULL], axis=0, keepdims=True)
        scale = lax.rsqrt(square / FULL + EPSILON) / (FULL * SOFTMAX_TEMP)
        logs = jnp.log(jnp.maximum(found[FULL : FULL + 1], 1.0))
        for i in range(width // LANE):
            row_scale[pl.ds(group0 + i, 1), :] = scale[:, i * LANE : (i + 1) * LANE]
            row_log[pl.ds(group0 + i, 1), :] = logs[:, i * LANE : (i + 1) * LANE]

    def fetch(h, carry):
        hot = jnp.concatenate([picked(2 * h), picked(2 * h + 1)], axis=1)
        keep(dot(cat_t[...], hot), pl.multiple_of(h * 256, 256), 256, 2 * h)
        return carry

    lax.fori_loop(0, GROUPS // 2, fetch, 0)
    keep(dot(cat_t[...], picked(GROUPS)), GROUPS * LANE, LANE, GROUPS)
    start_ch(X_ROWS, lambda p: rows_send.at[p], rows_all)
    rows_all[me_c] = rows_send[me_c]

    wait_ch(X_SIG, lambda p: sig_send.at[p], sig_all)
    wait_ch(X_WGATE, lambda p: wg_own, wg_all)
    gate_t[...] = dot(wg_all[...].reshape(FULL, FULL), sig_all[...].reshape(FULL, LANE))
    wait_ch(X_WOUT, lambda p: w_out, wo_all)
    wo_t[...] = wo_all[...].reshape(FULL, FULL).T

    wait_seq(X_BACK, lambda p: msg2.at[p], rcv2)
    rf[...] = rcv2[...].astype(F32)
    msgf[...] = rf[...].reshape(S * 32, LANE)
    diag = iota((CH, CH), 0) == iota((CH, CH), 1)
    gain_col = jnp.sum(jnp.where(diag, gain[...], 0.0), axis=1, keepdims=True)
    for q in range(8):
        conv = jnp.concatenate(
            [msgf[pl.ds(k * 8 + q, S, stride=32), :] for k in range(3)], axis=0
        )
        mix_send[q] = (conv + gain_col * sig_send[q].astype(F32)).astype(BF16)
    start_ch(X_MIX, lambda p: mix_send.at[p], mix_all)
    mix_all[me_c] = mix_send[me_c]
    wait_ch(X_MIX, lambda p: mix_send.at[p], mix_all)
    mix = mix_all[...].reshape(FULL, LANE).astype(F32) * gate_t[...]
    lo_send[...] = dot(wo_t[...], mix.astype(BF16)).astype(BF16).reshape(C, CH, LANE)
    start_ch(X_OUT, lambda p: lo_send.at[p], lo_all)
    lo_all[me_c] = lo_send[me_c]

    tok_pos = spos[...]
    pos_in = tok_pos >> 2
    where_in = ((pos_in >> 7) * 4 + (tok_pos & 3)) * LANE + (pos_in & 127)
    pick = onehot(iota((TOK, LANE), 0) == where_in)

    wait_ch(X_OUT, lambda p: lo_send.at[p], lo_all)
    lo_t = jnp.concatenate([lo_all[q] for q in range(8)], axis=1)
    q_own[...] = dot(lo_t, pick).astype(BF16)
    start_seq(X_QUERY, lambda p: q_own, q_all)
    q_all[me_s] = q_own[...]
    out_ref[...] = dot(perm[...], lo_t, 1, 1).astype(BF16)

    wait_ch(X_TABLE, lambda p: tab_own, tab_all)
    pair_ids = iota((2 * LANE, LANE), 0)
    block_ids = iota((LANE, LANE), 0)

    def slots(g, carry):
        for c in range(C):
            entry = tab_all[c, pl.ds(g, 1), :]
            target = jnp.where(entry < 0, -1, (entry & 127) + jnp.where(lane_row < NEG, 0, LANE))
            ohp[g, :, c * LANE : (c + 1) * LANE] = onehot(pair_ids == target)
        return carry

    lax.fori_loop(0, GROUPS, slots, 0)

    def target_slots(b, carry):
        rows = pl.ds(pl.multiple_of(b * LANE, LANE), LANE)
        for c in range(C):
            entry = tab_all[c, GROUPS : GROUPS + 1, :]
            ours = (entry >= 0) & ((lane_row >> 1) == b)
            target = jnp.where(ours, entry & 127, -1)
            oht[rows, c * LANE : (c + 1) * LANE] = onehot(block_ids == target)
        return carry

    lax.fori_loop(0, S, target_slots, 0)

    wait_ch(X_ROWS, lambda p: rows_send.at[p], rows_all)
    wait_seq(X_QUERY, lambda p: q_own, q_all)
    part[...] = jnp.zeros_like(part)

    def score(query, lane0, group):
        for c in range(C):
            one = query[:, c * LANE : (c + 1) * LANE]
            rows = rows_all[c, :, pl.ds(lane0, LANE)].astype(F32)
            part[c, pl.ds(group, 1), :] = jnp.sum(one * rows, axis=0, keepdims=True)
            part[c, pl.ds(24 + group, 1), :] = jnp.sum(one * one, axis=0, keepdims=True)

    def pair(g, carry):
        both = jnp.concatenate([q_all[2 * g], q_all[2 * g + 1]], axis=1)
        score(dot(both, ohp[g]), pl.multiple_of(g * LANE, LANE), g)
        return carry

    lax.fori_loop(0, GROUPS, pair, 0)

    def gather_targets(g, held):
        both = jnp.concatenate([q_all[2 * g], q_all[2 * g + 1]], axis=1)
        return held + dot(both, oht[pl.ds(pl.multiple_of(g * 256, 256), 256), :])

    score(
        lax.fori_loop(0, S // 2, gather_targets, jnp.zeros((CH, C * LANE), F32)),
        GROUPS * LANE,
        GROUPS,
    )
    start_ch(X_PART, lambda p: part.at[p], part_all)
    part_all[me_c] = part[me_c]
    wait_ch(X_PART, lambda p: part.at[p], part_all)
    whole = jnp.sum(part_all[...], axis=0)
    query_scale = lax.rsqrt(whole[24:48] / FULL + EPSILON)
    logit = whole[0:24] * query_scale * row_scale[...] - row_log[...]
    filled = tab_own[...] >= 0
    exp_parts = jnp.concatenate(
        split_parts(jnp.where(filled, jnp.exp(logit), 0.0)[0:GROUPS], 2), axis=0
    )
    tgt_parts = jnp.concatenate(
        split_parts(
            jnp.broadcast_to(jnp.where(filled, logit, 0.0)[GROUPS : GROUPS + 1], (16, LANE)), 3
        ),
        axis=0,
    )
    sums[...] = jnp.zeros_like(sums)
    own_lanes = pl.ds(pl.multiple_of(me_c * LANE, LANE), LANE)
    row32 = iota((2 * GROUPS, 1), 0)

    def totals(g, carry):
        found = dot(exp_parts, ohp[g, :, own_lanes], 1, 1)
        both = jnp.sum(jnp.where((row32 & 15) == g, found, 0.0), axis=0, keepdims=True)
        sums[2 * g, 0:1, :] = both[:, 0:LANE]
        sums[2 * g + 1, 0:1, :] = both[:, LANE:]
        targets = dot(
            tgt_parts, oht[pl.ds(pl.multiple_of(g * 256, 256), 256), own_lanes], 1, 1
        )
        joined = targets[0:1] + targets[16:17] + targets[32:33]
        sums[2 * g, 1:2, :] = joined[:, 0:LANE]
        sums[2 * g + 1, 1:2, :] = joined[:, LANE:]
        return carry

    lax.fori_loop(0, GROUPS, totals, 0)
    start_seq(X_SUMS, lambda p: sums.at[p], sums_all)
    sums_all[me_s] = sums[me_s]
    wait_seq(X_SUMS, lambda p: sums.at[p], sums_all)
    fin[...] = jnp.sum(sums_all[...], axis=0)
    start_ch(X_FIN, lambda p: fin, fin_all)
    fin_all[me_c] = fin[...]
    wait_ch(X_FIN, lambda p: fin, fin_all)
    last = jnp.sum(fin_all[...], axis=0)
    target_logit = last[1:2]
    loss_ref[...] = jnp.log(jnp.exp(target_logit) + last[0:1]) - target_logit

    sent_seq(X_CONV, lambda p: msg1.at[p], rcv1)
    sent_seq(X_REQ, lambda p: req_msg.at[p], req_all)
    sent_seq(X_BACK, lambda p: msg2.at[p], rcv2)
    sent_seq(X_QUERY, lambda p: q_own, q_all)
    sent_seq(X_SUMS, lambda p: sums.at[p], sums_all)
    sent_ch(X_SIG, lambda p: sig_send.at[p], sig_all)
    sent_ch(X_WGATE, lambda p: wg_own, wg_all)
    sent_ch(X_WOUT, lambda p: w_out, wo_all)
    sent_ch(X_TABLE, lambda p: tab_own, tab_all)
    sent_ch(X_ROWS, lambda p: rows_send.at[p], rows_all)
    sent_ch(X_MIX, lambda p: mix_send.at[p], mix_all)
    sent_ch(X_OUT, lambda p: lo_send.at[p], lo_all)
    sent_ch(X_PART, lambda p: part.at[p], part_all)
    sent_ch(X_FIN, lambda p: fin, fin_all)


def per_device(
    signal,
    filter_taps,
    skip_gain,
    w_gate,
    w_out,
    catalogue,
    item_draw_counts,
    sampled_pos,
    neg_owner,
    neg_row,
    target_owner,
    target_row,
):
    vmem = pl.BlockSpec(memory_space=pltpu.VMEM)
    scratch = [
        ((TOK, TOK), BF16),
        ((C, CH, LANE), BF16),
        ((C, CH, LANE), BF16),
        ((S * 32, LANE), F32),
        ((S, 32, LANE), BF16),
        ((S, 32, LANE), BF16),
        ((S, 32, LANE), F32),
        ((272, LANE), F32),
        ((256, 512), BF16),
        ((256, LANE), F32),
        ((S, 32, LANE), BF16),
        ((S, 32, LANE), BF16),
        ((CH, FULL), BF16),
        ((C, CH, FULL), BF16),
        ((C, CH, FULL), BF16),
        ((FULL, FULL), BF16),
        ((FULL, LANE), F32),
        ((C, CH, LANE), BF16),
        ((C, CH, LANE), BF16),
        ((C, CH, LANE), BF16),
        ((C, CH, LANE), BF16),
        ((CH, LANE), BF16),
        ((S, CH, LANE), BF16),
        ((S, 8, LANE), I32),
        ((S, 8, LANE), I32),
        ((64 * S, LANE), BF16),
        ((64 * S, LANE), F32),
        ((64 * S, LANE), F32),
        ((LANE, 64 * LANE), BF16),
        ((LANE, 64 * LANE), BF16),
        ((24, LANE), I32),
        ((C, 24, LANE), I32),
        ((FULL + 16, ITEMS), BF16),
        ((C, CH, SLOTS), BF16),
        ((C, CH, SLOTS), BF16),
        ((24, LANE), F32),
        ((24, LANE), F32),
        ((GROUPS, 2 * LANE, C * LANE), BF16),
        ((S * LANE, C * LANE), BF16),
        ((C, 48, LANE), F32),
        ((C, 48, LANE), F32),
        ((S, 8, LANE), F32),
        ((S, 8, LANE), F32),
        ((8, LANE), F32),
        ((C, 8, LANE), F32),
    ]
    layer_out, loss = pl.pallas_call(
        body,
        out_shape=(
            jax.ShapeDtypeStruct((TOK, CH), BF16),
            jax.ShapeDtypeStruct((1, LANE), F32),
        ),
        in_specs=[vmem] * 12,
        out_specs=(vmem, vmem),
        scratch_shapes=[pltpu.VMEM(shape, kind) for shape, kind in scratch]
        + [pltpu.SemaphoreType.DMA((14, S)), pltpu.SemaphoreType.DMA((14, S))],
        compiler_params=pltpu.CompilerParams(
            collective_id=0, has_side_effects=True, vmem_limit_bytes=60 * 1024 * 1024
        ),
        cost_estimate=pl.CostEstimate(
            flops=20_000_000_000, bytes_accessed=5_000_000, transcendentals=10_000
        ),
    )(
        signal.reshape(TOK, CH),
        filter_taps,
        skip_gain.reshape(1, CH),
        w_gate,
        w_out,
        catalogue,
        item_draw_counts.reshape(1, ITEMS),
        sampled_pos.reshape(1, LANE),
        neg_owner.reshape(64, LANE),
        neg_row.reshape(64, LANE),
        target_owner.reshape(1, LANE),
        target_row.reshape(1, LANE),
    )
    return layer_out.reshape(256, 4, CH), loss.reshape(LANE)


def solution(mesh):
    placed = (
        P("seq", None, "ch"),
        P("seq", "ch"),
        P("ch"),
        P(None, "ch"),
        P("ch", None),
        P(("seq", "ch"), None),
        P(("seq", "ch")),
        P("seq"),
        P("seq", None, None),
        P("seq", None),
        P("seq", None),
        P("seq"),
    )
    return jax.shard_map(
        per_device,
        mesh=mesh,
        in_specs=placed,
        out_specs=(P("seq", None, "ch"), P("seq")),
        check_vma=False,
    )
```

time: 1280 us -> 158 us (0.12)
  local copies, waits for them, and re-layouts: 513 us -> 11.1 us
  starting transfers between devices: 468 us -> 0 us
  waiting for transfers between devices: 204 us -> 0 us
  Pallas kernels: 0 us -> 146 us
  matrix products: 41.1 us -> 0 us
  other arithmetic: 28 us -> 0 us
  between operations: 14.8 us -> 0.65 us
    all_to_all x15 -> x0, starting transfers between devices: 468 us -> none  [the longest x1 379 us: per_device(): lax.all_to_all(fetched, 'seq', split_axis=0, concat_axis=0, tiled=True)]
    gather x5 -> x0, local copies, waits for them, and re-layouts: 395 us -> none  [the longest x3 308 us: per_device(): jnp.take(table, rows, axis=0)]
    pallas_call x0 -> x1, Pallas kernels: none -> 146 us  [per_device(): pl.pallas_call(body, out_shape=(jax.ShapeDtypeStruct((TOK, CH), BF16), ja...]
    all_to_all x15 -> x0, waiting for transfers between devices: 112 us -> none  [the longest x1 17.9 us: per_device(): lax.all_to_all(lax.all_to_all(fetched, 'seq', split_axis=0, concat_axis=0...]
    scatter x4 -> x0, local copies, waits for them, and re-layouts: 63 us -> none  [the longest x2 31.5 us: per_device(): request.at[neg_flat].set(neg_row.reshape(pos_dev * neg_count)).at[tgt_flat]]
    psum x1 -> x0, waiting for transfers between devices: 55.3 us -> none  [per_device(): lax.psum(slot_square.astype(jnp.bfloat16), 'ch').astype(jnp.float32)]
    dot_general x24 -> x0, matrix products: 41.1 us -> none  [the longest x2 5.38 us: second_section(): jnp.einsum('kn,jnb->jkb', sin_full, imag_part, precision=HIGHEST)]
    all_gather x1 -> x0, waiting for transfers between devices: 35.9 us -> none  [per_device(): lax.all_gather(signal, 'ch', axis=2, tiled=True)]
  transfers between devices with their start and end apart: 18 -> 0, of which waited for: 13 -> 0; matrix products, arithmetic and copies ran while one was open for 41% -> 0% of each run, Pallas kernels for 0% -> 0%
where the time goes in v1:
time: 158 us
  Pallas kernels  146 us (92%)
  local copies, waits for them, and re-layouts  11.1 us (7%)
    pallas_call x1, Pallas kernels, per_device(): pl.pallas_call(body, out_shape=(jax.ShapeDtypeStruct((TOK, CH), BF16), ja...  146 us
    unnamed x7, local copies, waits for them, and re-layouts  9.74 us

profile of v1, /device:TPU:1, one launch (start us, length us, event | category | flops | bytes accessed | tf_op | source)
XLA Modules:
  0.0 157.9 jit_solution(14697555000992725207)
XLA Ops:
  0.6 0.8 copy.21
  1.5 0.7 reshape.38.nown
  2.2 0.8 copy.22
  3.0 0.7 reshape.39.nrow
  3.7 1.6 %copy.23.taps = f32[256,96]{1,0:T(8,128)} copy(f32[256,96]{0,1:T(8,128)} %param.13) | data formatting | bytes 196608 | tf_op args[1]
  5.3 1.7 %copy.24.w_gate = bf16[768,96]{1,0:T(8,128)(2,1)} copy(bf16[768,96]{0,1:T(8,128)(2,1)} %param.15) | data formatting | bytes 294912 | tf_op args[3]
  7.1 1.8 %copy.20 = bf16[256,4,96]{2,1,0:T(4,128)(2,1)} copy(bf16[256,4,96]{0,2,1:T(8,128)(2,1)} %param.12) | data formatting | bytes 393216 | tf_op args[0]
  8.9 146.1 %shard_map.131 = (bf16[1024,96]{1,0:T(8,128)(2,1)}, f32[1,128]{1,0:T(1,128)}) custom-call(bf16[1024,96]{1,0:T(8,128)(2,1)} %bitcast.11, f32[256,96]{1,0:T(8,128)} %copy.23.taps, f32[1,96]{1,0:T(1,128)} %bitcast.13, bf16[768,96]{1,0:T(8,128)(2,1)} %copy.24.w_gate, bf16[96,768]{1,0:T(8,128)(2,1)} %w_out.1, bf16[2048,768]{1,0:T(8,128)(2,1)} %cat.1, ...), custom_call_target="tpu_custom_call" | custom-call | flops 20000000000 | bytes 5000000 | tf_op jit(solution)/shard_map/pallas_call | solution.py:573
  155.0 1.8 %copy.25 = bf16[256,4,96]{0,2,1:T(8,128)(2,1)} copy(bf16[256,4,96]{2,1,0:T(4,128)(2,1)} %bitcast.10) | data formatting | bytes 393216
  156.8 1.1 copy.27

commit v2 on v1

v2 whole, which is shorter than its diff:
```python
import jax
import jax.numpy as jnp
from jax import lax
from jax.experimental import pallas as pl
from jax.experimental.pallas import tpu as pltpu
from jax.sharding import PartitionSpec as P

SOFTMAX_TEMP = 0.02
EPSILON = 1e-06
MESH = pl.DeviceIdType.MESH
BF16 = jnp.bfloat16
F32 = jnp.float32
I32 = jnp.int32

S = 32
C = 8
LANE = 128
CH = 96
FULL = CH * C
TOK = 1024
NEG = 64
GROUPS = 16
SLOTS = (GROUPS + 1) * LANE
ITEMS = 2048

(
    X_CONV,
    X_BACK,
    X_QUERY,
    X_FORWARD,
    X_SUMS,
    X_SIG,
    X_WGATE,
    X_WOUT,
    X_WGATE_MATE,
    X_WOUT_MATE,
    X_TABLE,
    X_MIX,
    X_OUT,
    X_PART,
    X_FIN,
    X_ROWS,
) = range(16)
CHUNKS = GROUPS // 2 + 1
EXCHANGES = X_ROWS + CHUNKS
SIDE = 4
TGT_LANES = (0, 16, 64, 80)
TGT_BLOCKS = tuple(tuple(range(first, first + 16, 2)) for first in (1, 17, 0, 16))


def iota(shape, dim):
    return lax.broadcasted_iota(I32, shape, dim)


def onehot(mask):
    return jnp.where(mask, 1.0, 0.0).astype(BF16)


def dot(a, b, ca=1, cb=0):
    return lax.dot_general(a, b, (((ca,), (cb,)), ((), ())), preferred_element_type=F32)


def split_parts(value, count):
    parts = []
    for _ in range(count):
        piece = value.astype(BF16)
        parts.append(piece)
        value = value - piece.astype(F32)
    return parts


def body(
    sig,
    taps_t,
    gain,
    wg_own,
    w_out,
    cat_hbm,
    cnt,
    spos,
    nown,
    nrow,
    town,
    trow,
    out_ref,
    loss_ref,
    cat,
    sig_send,
    sig_all,
    msgf,
    msg1,
    rcv1,
    rf,
    xpad,
    x4,
    acc,
    msg2,
    rcv2,
    wg_all,
    wo_all,
    wo_t,
    gate_t,
    mix_send,
    mix_all,
    lo_send,
    lo_all,
    q_own,
    q_all,
    ohs,
    inner,
    total,
    keys,
    vals,
    tab_own,
    tab_all,
    tab_t,
    cat_t,
    rows_send,
    rows_all,
    row_scale,
    row_log,
    ohp,
    oht,
    slot_pos,
    part,
    part_all,
    sums,
    sums_all,
    fin,
    fin_all,
    send_sem,
    recv_sem,
    cat_sem,
):
    me_s = lax.axis_index("seq")
    me_c = lax.axis_index("ch")

    def seq_copy(x, peer, src, dst):
        return pltpu.make_async_remote_copy(
            src_ref=src,
            dst_ref=dst,
            send_sem=send_sem.at[x, peer],
            recv_sem=recv_sem.at[x, me_s],
            device_id=(peer, me_c),
            device_id_type=MESH,
        )

    def ch_copy(x, peer, src, dst):
        return pltpu.make_async_remote_copy(
            src_ref=src,
            dst_ref=dst,
            send_sem=send_sem.at[x, peer],
            recv_sem=recv_sem.at[x, me_c],
            device_id=(me_s, peer),
            device_id_type=MESH,
        )

    def over(n, me, fn):
        def step(d, carry):
            fn(lax.rem(me + d, n))
            return carry

        lax.fori_loop(1, n, step, 0)

    def start_seq(x, src_of, dst):
        over(S, me_s, lambda peer: seq_copy(x, peer, src_of(peer), dst.at[me_s]).start())

    def start_ch(x, src_of, dst):
        over(C, me_c, lambda peer: ch_copy(x, peer, src_of(peer), dst.at[me_c]).start())

    def wait_from(x, peer, src, dst, device):
        pltpu.make_async_remote_copy(
            src_ref=src,
            dst_ref=dst,
            send_sem=send_sem.at[x, peer],
            recv_sem=recv_sem.at[x, peer],
            device_id=device,
            device_id_type=MESH,
        ).wait_recv()

    def wait_seq(x, src_of, dst):
        over(S, me_s, lambda peer: wait_from(x, peer, src_of(peer), dst.at[peer], (peer, me_c)))

    def wait_ch(x, src_of, dst):
        over(C, me_c, lambda peer: wait_from(x, peer, src_of(peer), dst.at[peer], (me_s, peer)))

    def sent_seq(x, src_of, dst):
        over(S, me_s, lambda peer: seq_copy(x, peer, src_of(peer), dst.at[me_s]).wait_send())

    def sent_ch(x, src_of, dst):
        over(C, me_c, lambda peer: ch_copy(x, peer, src_of(peer), dst.at[me_c]).wait_send())

    barrier = pltpu.get_barrier_semaphore()

    def greet_seq(peer):
        pl.semaphore_signal(barrier, inc=1, device_id=(peer, me_c), device_id_type=MESH)

    def greet_ch(peer):
        pl.semaphore_signal(barrier, inc=1, device_id=(me_s, peer), device_id_type=MESH)

    over(S, me_s, greet_seq)
    over(C, me_c, greet_ch)

    cat_copy = pltpu.make_async_copy(cat_hbm, cat, cat_sem)
    cat_copy.start()

    upper = onehot(iota((LANE, LANE), 0) < iota((LANE, LANE), 1))
    ones = jnp.ones((LANE, LANE), BF16)
    owner_ids = iota((S, LANE), 0)

    def own_onehot(owners):
        mine = jnp.where((owners & 7) == me_c, owners >> 3, -1)
        return jnp.where(owner_ids == mine, 1.0, 0.0)

    def mark(m, carry):
        ohs[pl.ds(pl.multiple_of(m * S, S), S), :] = own_onehot(nown[m]).astype(BF16)
        return carry

    lax.fori_loop(0, 64, mark, 0, unroll=4)
    inner[...] = dot(ohs[...], upper)
    total[...] = dot(ohs[...], ones)
    key_ids = iota((LANE, LANE), 0).astype(F32)
    lane_row = iota((1, LANE), 1)

    def key_of(hot, rank, offset):
        found = jnp.sum(hot * (rank + 1.0), axis=0, keepdims=True)
        place = jnp.where(found > 0.5, found - 1.0 + offset, -1.0)
        return jnp.where(key_ids == place, 1.0, 0.0).astype(BF16)

    def value_of(hot, rows):
        high = (rows >> 8).astype(F32)
        low = (rows & 255).astype(F32)
        pieces = [hot * high, hot * low, hot * lane_row.astype(F32), hot]
        return jnp.concatenate(pieces, axis=0).astype(BF16)

    odd = lax.rem(me_s, 2)
    neg_offset = (odd * NEG).astype(F32)
    tgt_offset = ((1 - odd) * NEG + me_s - odd).astype(F32)

    def place(m, before):
        rows = pl.ds(pl.multiple_of(m * S, S), S)
        lanes = pl.ds(pl.multiple_of(m * LANE, LANE), LANE)
        hot = ohs[rows, :].astype(F32)
        keys[:, lanes] = key_of(hot, inner[rows, :] + before, neg_offset)
        vals[:, lanes] = value_of(hot, nrow[pl.ds(m, 1), :])
        return before + total[rows, :]

    lax.fori_loop(0, 64, place, jnp.zeros((S, LANE), F32), unroll=4)
    hot = own_onehot(town[...])
    rank = dot(hot.astype(BF16), upper)
    found = dot(vals[...], keys[...], 1, 1) + dot(
        value_of(hot, trow[...]), key_of(hot, rank, tgt_offset), 1, 1
    )
    high, low, pos, filled = (found[i * S : (i + 1) * S].astype(I32) for i in range(4))
    entry = (high * 256 + low) * LANE + pos
    entry_high = jnp.where(filled > 0, (entry >> 9) - 256, 1024).astype(F32)
    entry_low = jnp.where(filled > 0, (entry & 511) - 256, 0).astype(F32)

    for q in range(8):
        piece = sig[q % 4, :, (q // 4) * LANE : (q // 4 + 1) * LANE]
        sig_send[q] = piece
        for k in range(3):
            msgf[pl.ds(k * 8 + q, S, stride=32), :] = piece[k * 32 : (k + 1) * 32].astype(F32)
    for il in range(2):
        for k in range(3):
            msgf[pl.ds(24 + 2 * k + il, S, stride=32), :] = taps_t[
                k * 32 : (k + 1) * 32, il * LANE : (il + 1) * LANE
            ]
    msgf[pl.ds(30, S, stride=32), :] = entry_high
    msgf[pl.ds(31, S, stride=32), :] = entry_low
    msg1[...] = msgf[...].reshape(S, 32, LANE).astype(BF16)

    pl.semaphore_wait(barrier, S - 1 + C - 1)

    start_seq(X_CONV, lambda p: msg1.at[p], rcv1)
    rcv1[me_s] = msg1[me_s]
    start_ch(X_SIG, lambda p: sig_send.at[p], sig_all)
    sig_all[me_c] = sig_send[me_c]

    core = lax.rem(me_c, 2)
    mate = me_c + 1 - 2 * core

    def over_x(fn):
        def step(d, carry):
            fn(lax.rem(me_c + 2 * d, C))
            return carry

        lax.fori_loop(1, SIDE, step, 0)

    def start_weight(x, src, dst):
        over_x(lambda peer: ch_copy(x, peer, src, dst.at[me_c]).start())
        ch_copy(x, mate, src, dst.at[me_c]).start()
        dst[me_c] = src[...]

    def mate_copy(x, x_mate, peer, dst):
        return pltpu.make_async_remote_copy(
            src_ref=dst.at[peer],
            dst_ref=dst.at[peer],
            send_sem=send_sem.at[x_mate, peer],
            recv_sem=recv_sem.at[x, peer],
            device_id=(me_s, mate),
            device_id_type=MESH,
        )

    def pass_weight(x, x_mate, src, dst):
        def fn(peer):
            wait_from(x, peer, src, dst.at[peer], (me_s, peer))
            mate_copy(x, x_mate, peer, dst).start()

        over_x(fn)

    def wait_weight(x, src, dst):
        wait_from(x, mate, src, dst.at[mate], (me_s, mate))

        def fn(peer):
            other = peer + 1 - 2 * core
            wait_from(x, other, src, dst.at[other], (me_s, mate))

        over_x(fn)

    def sent_weight(x, x_mate, src, dst):
        over_x(lambda peer: ch_copy(x, peer, src, dst.at[me_c]).wait_send())
        ch_copy(x, mate, src, dst.at[me_c]).wait_send()
        over_x(lambda peer: mate_copy(x, x_mate, peer, dst).wait_send())

    start_weight(X_WGATE, wg_own, wg_all)
    start_weight(X_WOUT, w_out, wo_all)

    cat_copy.wait()

    def turn(i, carry):
        span = pl.ds(pl.multiple_of(i * 256, 256), 256)
        cat_t[0:FULL, span] = cat[span, :].T
        return carry

    lax.fori_loop(0, ITEMS // 256, turn, 0)
    cat_t[FULL : FULL + 16, :] = jnp.broadcast_to(cnt[...].astype(F32), (16, ITEMS)).astype(BF16)

    wait_seq(X_CONV, lambda p: msg1.at[p], rcv1)
    rf[...] = rcv1[...].astype(F32)
    xpad[0:16, :] = jnp.zeros((16, LANE), F32)
    later = iota((LANE, LANE), 1) >= iota((LANE, LANE), 0)
    for k in range(3):
        xpad[16:272, :] = rf[:, k * 8 : (k + 1) * 8, :].reshape(256, LANE)
        x4[...] = jnp.concatenate(
            [xpad[16 - 4 * j : 272 - 4 * j, :] for j in range(4)], axis=1
        ).astype(BF16)
        acc[...] = jnp.zeros_like(acc)
        prev = jnp.zeros((LANE, LANE), F32)
        for e in range(16):
            tiles = []
            for j in range(4):
                d = 4 * e + j
                row = 24 + 2 * k + d % 2
                chunk = jnp.broadcast_to(rf[d // 2, row : row + 1, :], (LANE, LANE))
                turned = pltpu.roll(chunk, 0, 1, stride=1, stride_axis=0)
                tiles.append(jnp.where(later, turned, prev).astype(BF16))
                prev = turned
            taps_tile = jnp.concatenate(tiles, axis=0)
            acc[16 * e :, :] += dot(x4[0 : 256 - 16 * e, :], taps_tile)
        for s in range(S):
            msgf[s * 32 + k * 8 : s * 32 + k * 8 + 8, :] = acc[s * 8 : s * 8 + 8, :]
    msg2[...] = msgf[...].reshape(S, 32, LANE).astype(BF16)
    start_seq(X_BACK, lambda p: msg2.at[p], rcv2)
    rcv2[me_s] = msg2[me_s]

    asked_high = rf[:, 30, :].astype(I32)
    asked_low = rf[:, 31, :].astype(I32)
    asked = jnp.where(asked_high < 512, (asked_high + 256) * 512 + asked_low + 256, -1)
    asked = asked.reshape(GROUPS, 2, LANE)
    even_half, odd_half = asked[:, 0, :], asked[:, 1, :]
    first_half = iota((GROUPS, LANE), 1) < NEG
    tab_own[...] = jnp.full(tab_own.shape, -1, I32)
    tab_own[0:GROUPS, :] = jnp.where(first_half, even_half, odd_half)
    tab_own[GROUPS : GROUPS + 1, :] = jnp.max(
        jnp.where(first_half, odd_half, even_half), axis=0, keepdims=True
    )
    start_ch(X_TABLE, lambda p: tab_own, tab_all)
    tab_all[me_c] = tab_own[...]
    row_scale[...] = jnp.zeros_like(row_scale)
    row_log[...] = jnp.zeros_like(row_log)
    item_ids = iota((ITEMS, LANE), 0)

    def picked(group):
        return onehot(item_ids == (tab_own[pl.ds(group, 1), :] >> 7))

    def keep(found, width, group0):
        for i in range(width // LANE):
            lanes = slice(i * LANE, (i + 1) * LANE)
            for c in range(C):
                rows_send[group0 + i, c] = found[c * CH : (c + 1) * CH, lanes].astype(BF16)
            rows_all[group0 + i, me_c] = rows_send[group0 + i, me_c]
        square = jnp.sum(found[0:FULL] * found[0:FULL], axis=0, keepdims=True)
        scale = lax.rsqrt(square / FULL + EPSILON) / (FULL * SOFTMAX_TEMP)
        logs = jnp.log(jnp.maximum(found[FULL : FULL + 1], 1.0))
        for i in range(width // LANE):
            row_scale[pl.ds(group0 + i, 1), :] = scale[:, i * LANE : (i + 1) * LANE]
            row_log[pl.ds(group0 + i, 1), :] = logs[:, i * LANE : (i + 1) * LANE]

    def chunk_copy(h, peer):
        span = pl.ds(2 * h, 2)
        return ch_copy(X_ROWS + h, peer, rows_send.at[span, peer], rows_all.at[span, me_c])

    def target_copy(peer):
        x = X_ROWS + CHUNKS - 1
        return ch_copy(x, peer, rows_send.at[GROUPS, peer], rows_all.at[GROUPS, me_c])

    def fetch(first, last):
        def step(h, carry):
            hot = jnp.concatenate([picked(2 * h), picked(2 * h + 1)], axis=1)
            keep(dot(cat_t[...], hot), 256, 2 * h)
            over(C, me_c, lambda peer: chunk_copy(h, peer).start())
            return carry

        lax.fori_loop(first, last, step, 0)

    def fetch_targets():
        keep(dot(cat_t[...], picked(GROUPS)), LANE, GROUPS)
        over(C, me_c, lambda peer: target_copy(peer).start())

    def wait_rows():
        def step(h, carry):
            span = pl.ds(2 * h, 2)

            def fn(peer):
                src, dst = rows_send.at[span, peer], rows_all.at[span, peer]
                wait_from(X_ROWS + h, peer, src, dst, (me_s, peer))

            over(C, me_c, fn)
            return carry

        lax.fori_loop(0, CHUNKS - 1, step, 0)

        def last(peer):
            src, dst = rows_send.at[GROUPS, peer], rows_all.at[GROUPS, peer]
            wait_from(X_ROWS + CHUNKS - 1, peer, src, dst, (me_s, peer))

        over(C, me_c, last)

    def sent_rows():
        def step(h, carry):
            over(C, me_c, lambda peer: chunk_copy(h, peer).wait_send())
            return carry

        lax.fori_loop(0, CHUNKS - 1, step, 0)
        over(C, me_c, lambda peer: target_copy(peer).wait_send())

    fetch(0, 4)
    pass_weight(X_WGATE, X_WGATE_MATE, wg_own, wg_all)
    wait_ch(X_SIG, lambda p: sig_send.at[p], sig_all)

    wait_seq(X_BACK, lambda p: msg2.at[p], rcv2)
    rf[...] = rcv2[...].astype(F32)
    msgf[...] = rf[...].reshape(S * 32, LANE)
    diag = iota((CH, CH), 0) == iota((CH, CH), 1)
    gain_col = jnp.sum(jnp.where(diag, gain[...], 0.0), axis=1, keepdims=True)
    for q in range(8):
        conv = jnp.concatenate(
            [msgf[pl.ds(k * 8 + q, S, stride=32), :] for k in range(3)], axis=0
        )
        mix_send[q] = (conv + gain_col * sig_send[q].astype(F32)).astype(BF16)
    start_ch(X_MIX, lambda p: mix_send.at[p], mix_all)
    mix_all[me_c] = mix_send[me_c]
    pass_weight(X_WOUT, X_WOUT_MATE, w_out, wo_all)

    wait_weight(X_WGATE, wg_own, wg_all)
    gate_t[...] = dot(wg_all[...].reshape(FULL, FULL), sig_all[...].reshape(FULL, LANE))
    fetch(4, 6)
    wait_weight(X_WOUT, w_out, wo_all)
    wo_t[...] = wo_all[...].reshape(FULL, FULL).T
    wait_ch(X_MIX, lambda p: mix_send.at[p], mix_all)
    mix = mix_all[...].reshape(FULL, LANE).astype(F32) * gate_t[...]
    lo_send[...] = dot(wo_t[...], mix.astype(BF16)).astype(BF16).reshape(C, CH, LANE)
    start_ch(X_OUT, lambda p: lo_send.at[p], lo_all)
    lo_all[me_c] = lo_send[me_c]

    fetch(6, 8)
    tok_pos = spos[...]
    pos_in = tok_pos >> 2
    where_in = ((pos_in >> 7) * 4 + (tok_pos & 3)) * LANE + (pos_in & 127)
    pick = onehot(iota((TOK, LANE), 0) == where_in)

    wait_ch(X_OUT, lambda p: lo_send.at[p], lo_all)
    lo_t = jnp.concatenate([lo_all[q] for q in range(8)], axis=1)
    q_own[...] = dot(lo_t, pick).astype(BF16)

    me_z, me_y = me_s // SIDE, lax.rem(me_s, SIDE)
    layers = S // SIDE

    def block_to(x, slot, peer, src, block):
        return pltpu.make_async_remote_copy(
            src_ref=src,
            dst_ref=q_all.at[block],
            send_sem=send_sem.at[x, slot],
            recv_sem=recv_sem.at[X_QUERY, block],
            device_id=(peer, me_c),
            device_id_type=MESH,
        )

    def along_z(fn):
        def step(d, carry):
            fn(lax.rem(me_z + d, layers) * SIDE + me_y)
            return carry

        lax.fori_loop(1, layers, step, 0)

    def along_y(block, src, fn):
        def step(d, carry):
            peer = me_z * SIDE + lax.rem(me_y + d, SIDE)
            fn(block_to(X_FORWARD, d * layers + block // SIDE, peer, src, block))
            return carry

        lax.fori_loop(1, SIDE, step, 0)

    def take_block(block):
        wait_from(X_QUERY, block, q_own, q_all.at[block], (block, me_c))

    along_z(lambda peer: block_to(X_QUERY, peer, peer, q_own, me_s).start())
    along_y(me_s, q_own, lambda copy: copy.start())
    q_all[me_s] = q_own[...]
    for q in range(8):
        out_ref[q % 4, :, (q // 4) * LANE : (q // 4 + 1) * LANE] = lo_all[q]

    def go_on(block):
        take_block(block)
        along_y(block, q_all.at[block], lambda copy: copy.start())

    along_z(go_on)
    fetch_targets()

    wait_ch(X_TABLE, lambda p: tab_own, tab_all)
    pair_ids = iota((2 * LANE, LANE), 0)

    def slots(g, carry):
        for c in range(C):
            entry = tab_all[c, pl.ds(g, 1), :]
            target = jnp.where(entry < 0, -1, (entry & 127) + jnp.where(lane_row < NEG, 0, LANE))
            ohp[g, :, c * LANE : (c + 1) * LANE] = onehot(pair_ids == target)
        return carry

    lax.fori_loop(0, GROUPS, slots, 0)
    wide_ids = iota((8 * LANE, LANE), 0)
    part_of = lane_row >> 4
    for o, lane0 in enumerate(TGT_LANES):
        entry = jnp.full((1, LANE), -1, I32)
        for c in range(C):
            turned = pltpu.roll(tab_all[c, GROUPS : GROUPS + 1, :], (16 * c - lane0) % LANE, 1)
            entry = jnp.where(part_of == c, turned, entry)
        target = jnp.where(entry < 0, -1, ((lane_row & 15) >> 1) * LANE + (entry & 127))
        oht[o] = onehot(wide_ids == target)
    tab_t[...] = jnp.full(tab_t.shape, -1.0, F32)
    tab_t[0:24, :] = jnp.where(tab_own[...] < 0, -1, tab_own[...] & 127).astype(F32)
    columns = tab_t[...].T
    pos_ids = iota((LANE, LANE), 1).astype(F32)
    for g in range(GROUPS + 1):
        slot_pos[g] = onehot(columns[:, g : g + 1] == pos_ids)

    wait_rows()
    tgt_rows = []
    for lane0 in TGT_LANES:
        rows = jnp.zeros((CH, LANE), F32)
        for c in range(C):
            turned = pltpu.roll(rows_all[GROUPS, c].astype(F32), (16 * c - lane0) % LANE, 1)
            rows = jnp.where(part_of == c, turned, rows)
        tgt_rows.append(rows)
    part[...] = jnp.zeros_like(part)

    def rest_of_blocks(d, carry):
        y = lax.rem(me_y + d, SIDE)

        def step(z, inside):
            take_block(z * SIDE + y)
            return inside

        lax.fori_loop(0, layers, step, 0)
        return carry

    lax.fori_loop(1, SIDE, rest_of_blocks, 0)

    def pair(g, carry):
        both = jnp.concatenate([q_all[2 * g], q_all[2 * g + 1]], axis=1)
        query = dot(both, ohp[g])
        for c in range(C):
            one = query[:, c * LANE : (c + 1) * LANE]
            rows = rows_all[g, c].astype(F32)
            part[c, pl.ds(g, 1), :] = jnp.sum(one * rows, axis=0, keepdims=True)
            part[c, pl.ds(24 + g, 1), :] = jnp.sum(one * one, axis=0, keepdims=True)
        return carry

    lax.fori_loop(0, GROUPS, pair, 0, unroll=2)
    tgt_part = [[jnp.zeros((1, LANE), F32) for _ in range(2)] for _ in range(C)]
    for o, lane0 in enumerate(TGT_LANES):
        wide = jnp.concatenate([q_all[b] for b in TGT_BLOCKS[o]], axis=1)
        one = dot(wide, oht[o])
        for i, rows in enumerate((tgt_rows[o], one)):
            both = jnp.sum(one * rows, axis=0, keepdims=True)
            for c in range(C):
                turned = pltpu.roll(both, (lane0 - 16 * c) % LANE, 1)
                ours = (lane_row >= lane0) & (lane_row < lane0 + 16)
                tgt_part[c][i] = jnp.where(ours, turned, tgt_part[c][i])
    for c in range(C):
        part[c, GROUPS : GROUPS + 1, :] = tgt_part[c][0]
        part[c, 24 + GROUPS : 25 + GROUPS, :] = tgt_part[c][1]
    start_ch(X_PART, lambda p: part.at[p], part_all)
    part_all[me_c] = part[me_c]
    wait_ch(X_PART, lambda p: part.at[p], part_all)
    whole = jnp.sum(part_all[...], axis=0)
    query_scale = lax.rsqrt(whole[24:48] / FULL + EPSILON)
    logit = whole[0:24] * query_scale * row_scale[...] - row_log[...]
    filled = tab_own[...] >= 0
    exp_neg = jnp.where(filled, jnp.exp(logit), 0.0)[0:GROUPS]
    halves = [jnp.where(first_half, exp_neg, 0.0), jnp.where(first_half, 0.0, exp_neg)]
    exp_parts = jnp.concatenate([p for half in halves for p in split_parts(half, 2)], axis=0)
    tgt_logit = jnp.where(filled, logit, 0.0)[GROUPS : GROUPS + 1]
    block_of = 2 * ((lane_row & 63) >> 1) + jnp.where(lane_row < NEG, 1, 0)
    by_block = jnp.where(iota((S, LANE), 0) == block_of, tgt_logit, 0.0)
    tgt_parts = jnp.concatenate(split_parts(by_block, 3), axis=0)
    targets = dot(tgt_parts, slot_pos[GROUPS])
    targets = targets[0:S] + targets[S : 2 * S] + targets[2 * S : 3 * S]
    sums[...] = jnp.zeros_like(sums)
    sums[:, 1, :] = targets
    for g in range(GROUPS):
        found = dot(exp_parts, slot_pos[g])
        sums[2 * g, 0:1, :] = found[g : g + 1] + found[16 + g : 17 + g]
        sums[2 * g + 1, 0:1, :] = found[32 + g : 33 + g] + found[48 + g : 49 + g]
    start_seq(X_SUMS, lambda p: sums.at[p], sums_all)
    sums_all[me_s] = sums[me_s]
    wait_seq(X_SUMS, lambda p: sums.at[p], sums_all)
    fin[...] = jnp.sum(sums_all[...], axis=0)
    start_ch(X_FIN, lambda p: fin, fin_all)
    fin_all[me_c] = fin[...]
    wait_ch(X_FIN, lambda p: fin, fin_all)
    last = jnp.sum(fin_all[...], axis=0)
    target_logit = last[1:2]
    loss_ref[...] = jnp.log(jnp.exp(target_logit) + last[0:1]) - target_logit

    sent_seq(X_CONV, lambda p: msg1.at[p], rcv1)
    sent_seq(X_BACK, lambda p: msg2.at[p], rcv2)
    along_z(lambda peer: block_to(X_QUERY, peer, peer, q_own, me_s).wait_send())
    along_y(me_s, q_own, lambda copy: copy.wait_send())
    along_z(lambda block: along_y(block, q_all.at[block], lambda copy: copy.wait_send()))
    sent_seq(X_SUMS, lambda p: sums.at[p], sums_all)
    sent_ch(X_SIG, lambda p: sig_send.at[p], sig_all)
    sent_weight(X_WGATE, X_WGATE_MATE, wg_own, wg_all)
    sent_weight(X_WOUT, X_WOUT_MATE, w_out, wo_all)
    sent_ch(X_TABLE, lambda p: tab_own, tab_all)
    sent_rows()
    sent_ch(X_MIX, lambda p: mix_send.at[p], mix_all)
    sent_ch(X_OUT, lambda p: lo_send.at[p], lo_all)
    sent_ch(X_PART, lambda p: part.at[p], part_all)
    sent_ch(X_FIN, lambda p: fin, fin_all)


def per_device(
    signal,
    filter_taps,
    skip_gain,
    w_gate,
    w_out,
    catalogue,
    item_draw_counts,
    sampled_pos,
    neg_owner,
    neg_row,
    target_owner,
    target_row,
):
    vmem = pl.BlockSpec(memory_space=pltpu.VMEM)
    scratch = [
        ((ITEMS, FULL), BF16),
        ((C, CH, LANE), BF16),
        ((C, CH, LANE), BF16),
        ((S * 32, LANE), F32),
        ((S, 32, LANE), BF16),
        ((S, 32, LANE), BF16),
        ((S, 32, LANE), F32),
        ((272, LANE), F32),
        ((256, 512), BF16),
        ((256, LANE), F32),
        ((S, 32, LANE), BF16),
        ((S, 32, LANE), BF16),
        ((C, CH, FULL), BF16),
        ((C, CH, FULL), BF16),
        ((FULL, FULL), BF16),
        ((FULL, LANE), F32),
        ((C, CH, LANE), BF16),
        ((C, CH, LANE), BF16),
        ((C, CH, LANE), BF16),
        ((C, CH, LANE), BF16),
        ((CH, LANE), BF16),
        ((S, CH, LANE), BF16),
        ((64 * S, LANE), BF16),
        ((64 * S, LANE), F32),
        ((64 * S, LANE), F32),
        ((LANE, 64 * LANE), BF16),
        ((LANE, 64 * LANE), BF16),
        ((24, LANE), I32),
        ((C, 24, LANE), I32),
        ((LANE, LANE), F32),
        ((FULL + 16, ITEMS), BF16),
        ((GROUPS + 1, C, CH, LANE), BF16),
        ((GROUPS + 1, C, CH, LANE), BF16),
        ((24, LANE), F32),
        ((24, LANE), F32),
        ((GROUPS, 2 * LANE, C * LANE), BF16),
        ((len(TGT_LANES), 8 * LANE, LANE), BF16),
        ((GROUPS + 1, LANE, LANE), BF16),
        ((C, 48, LANE), F32),
        ((C, 48, LANE), F32),
        ((S, 8, LANE), F32),
        ((S, 8, LANE), F32),
        ((8, LANE), F32),
        ((C, 8, LANE), F32),
    ]
    layer_out, loss = pl.pallas_call(
        body,
        out_shape=(
            jax.ShapeDtypeStruct((4, CH, 256), BF16),
            jax.ShapeDtypeStruct((1, LANE), F32),
        ),
        in_specs=[vmem] * 5 + [pl.BlockSpec(memory_space=pl.ANY)] + [vmem] * 6,
        out_specs=(vmem, vmem),
        scratch_shapes=[pltpu.VMEM(shape, kind) for shape, kind in scratch]
        + [pltpu.SemaphoreType.DMA((EXCHANGES, S))] * 2
        + [pltpu.SemaphoreType.DMA(())],
        compiler_params=pltpu.CompilerParams(
            collective_id=0, has_side_effects=True, vmem_limit_bytes=60 * 1024 * 1024
        ),
        cost_estimate=pl.CostEstimate(
            flops=20_000_000_000, bytes_accessed=5_000_000, transcendentals=10_000
        ),
    )(
        signal.transpose(1, 2, 0),
        filter_taps.T,
        skip_gain.reshape(1, CH),
        w_gate.T,
        w_out,
        catalogue,
        item_draw_counts.reshape(1, ITEMS),
        sampled_pos.reshape(1, LANE),
        neg_owner.transpose(1, 2, 0),
        neg_row.T,
        target_owner.reshape(1, LANE),
        target_row.reshape(1, LANE),
    )
    return layer_out.transpose(2, 0, 1), loss.reshape(LANE)


def solution(mesh):
    placed = (
        P("seq", None, "ch"),
        P("seq", "ch"),
        P("ch"),
        P(None, "ch"),
        P("ch", None),
        P(("seq", "ch"), None),
        P(("seq", "ch")),
        P("seq"),
        P("seq", None, None),
        P("seq", None),
        P("seq", None),
        P("seq"),
    )
    return jax.shard_map(
        per_device,
        mesh=mesh,
        in_specs=placed,
        out_specs=(P("seq", None, "ch"), P("seq")),
        check_vma=False,
    )
```

time: 158 us -> 116 us (0.73)
  Pallas kernels: 146 us -> 113 us
  local copies, waits for them, and re-layouts: 11.1 us -> 2.75 us
    pallas_call x1, Pallas kernels: 146 us -> 113 us  [per_device(): pl.pallas_call(body, out_shape=(jax.ShapeDtypeStruct((4, CH, 256), BF16),...]
    unnamed x7 -> x2, local copies, waits for them, and re-layouts: 9.74 us -> 2.75 us
where the time goes in v2:
time: 116 us
  Pallas kernels  113 us (97%)
  local copies, waits for them, and re-layouts  2.75 us (2%)
    pallas_call x1, Pallas kernels, per_device(): pl.pallas_call(body, out_shape=(jax.ShapeDtypeStruct((4, CH, 256), BF16),...  113 us
    unnamed x2, local copies, waits for them, and re-layouts  2.75 us

profile of v2, /device:TPU:1, one launch (start us, length us, event | category | flops | bytes accessed | tf_op | source)
XLA Modules:
  0.0 116.3 jit_solution(15591476321911871440)
XLA Ops:
  0.6 112.9 %shard_map.131 = (bf16[4,96,256]{2,1,0:T(8,128)(2,1)}, f32[1,128]{1,0:T(1,128)}) custom-call(bf16[4,96,256]{2,1,0:T(8,128)(2,1)} %bitcast.13, f32[96,256]{1,0:T(8,128)} %bitcast.15, f32[1,96]{1,0:T(1,128)} %bitcast.19, bf16[96,768]{1,0:T(8,128)(2,1)} %bitcast.14, bf16[96,768]{1,0:T(8,128)(2,1)} %w_out.1, bf16[2048,768]{1,0:T(8,128)(2,1)} %cat_hbm.1, ...), custom_call_target="tpu_custom_call" | custom-call | flops 20000000000 | bytes 5000000 | tf_op jit(solution)/shard_map/pallas_call | solution.py:715
  113.6 1.6 %copy.16 = bf16[256,4,96]{0,2,1:T(8,128)(2,1)} copy(bf16[256,4,96]{0,2,1:T(8,128)(2,1)} %bitcast.12) | data formatting | bytes 393216
  115.2 1.1 copy.17

commit v3 on v2

--- a/solution.py
+++ b/solution.py
@@ -41,8 +41,9 @@
     X_FIN,
     X_ROWS,
 ) = range(16)
+X_LAYER = X_ROWS + GROUPS // 2 + 1
 CHUNKS = GROUPS // 2 + 1
-EXCHANGES = X_ROWS + CHUNKS
+EXCHANGES = X_LAYER + 8
 SIDE = 4
 TGT_LANES = (0, 16, 64, 80)
 TGT_BLOCKS = tuple(tuple(range(first, first + 16, 2)) for first in (1, 17, 0, 16))
@@ -135,25 +136,21 @@
     me_s = lax.axis_index("seq")
     me_c = lax.axis_index("ch")
 
-    def seq_copy(x, peer, src, dst):
+    def copy_to(x, device, src, dst, x_recv=None):
         return pltpu.make_async_remote_copy(
             src_ref=src,
             dst_ref=dst,
-            send_sem=send_sem.at[x, peer],
-            recv_sem=recv_sem.at[x, me_s],
-            device_id=(peer, me_c),
+            send_sem=send_sem.at[x],
+            recv_sem=recv_sem.at[x if x_recv is None else x_recv],
+            device_id=device,
             device_id_type=MESH,
         )
 
-    def ch_copy(x, peer, src, dst):
-        return pltpu.make_async_remote_copy(
-            src_ref=src,
-            dst_ref=dst,
-            send_sem=send_sem.at[x, peer],
-            recv_sem=recv_sem.at[x, me_c],
-            device_id=(me_s, peer),
-            device_id_type=MESH,
-        )
+    def arrived(x, like):
+        copy_to(x, (me_s, me_c), like, like).wait_recv()
+
+    def sent(x, like):
+        copy_to(x, (me_s, me_c), like, like).wait_send()
 
     def over(n, me, fn):
         def step(d, carry):
@@ -163,32 +160,22 @@
         lax.fori_loop(1, n, step, 0)
 
     def start_seq(x, src_of, dst):
-        over(S, me_s, lambda peer: seq_copy(x, peer, src_of(peer), dst.at[me_s]).start())
+        over(S, me_s, lambda p: copy_to(x, (p, me_c), src_of(p), dst.at[me_s]).start())
 
     def start_ch(x, src_of, dst):
-        over(C, me_c, lambda peer: ch_copy(x, peer, src_of(peer), dst.at[me_c]).start())
-
-    def wait_from(x, peer, src, dst, device):
-        pltpu.make_async_remote_copy(
-            src_ref=src,
-            dst_ref=dst,
-            send_sem=send_sem.at[x, peer],
-            recv_sem=recv_sem.at[x, peer],
-            device_id=device,
-            device_id_type=MESH,
-        ).wait_recv()
-
-    def wait_seq(x, src_of, dst):
-        over(S, me_s, lambda peer: wait_from(x, peer, src_of(peer), dst.at[peer], (peer, me_c)))
-
-    def wait_ch(x, src_of, dst):
-        over(C, me_c, lambda peer: wait_from(x, peer, src_of(peer), dst.at[peer], (me_s, peer)))
-
-    def sent_seq(x, src_of, dst):
-        over(S, me_s, lambda peer: seq_copy(x, peer, src_of(peer), dst.at[me_s]).wait_send())
-
-    def sent_ch(x, src_of, dst):
-        over(C, me_c, lambda peer: ch_copy(x, peer, src_of(peer), dst.at[me_c]).wait_send())
+        over(C, me_c, lambda p: copy_to(x, (me_s, p), src_of(p), dst.at[me_c]).start())
+
+    def wait_seq(x, dst):
+        arrived(x, dst.at[pl.ds(0, S - 1)])
+
+    def wait_ch(x, dst):
+        arrived(x, dst.at[pl.ds(0, C - 1)])
+
+    def sent_seq(x, dst):
+        sent(x, dst.at[pl.ds(0, S - 1)])
+
+    def sent_ch(x, dst):
+        sent(x, dst.at[pl.ds(0, C - 1)])
 
     barrier = pltpu.get_barrier_semaphore()
 
@@ -287,44 +274,24 @@
 
         lax.fori_loop(1, SIDE, step, 0)
 
-    def start_weight(x, src, dst):
-        over_x(lambda peer: ch_copy(x, peer, src, dst.at[me_c]).start())
-        ch_copy(x, mate, src, dst.at[me_c]).start()
+    def start_weight(x, x_mate, src, dst):
+        over_x(lambda p: copy_to(x, (me_s, p), src, dst.at[me_c]).start())
+        copy_to(x, (me_s, mate), src, dst.at[me_c], x_mate).start()
         dst[me_c] = src[...]
 
-    def mate_copy(x, x_mate, peer, dst):
-        return pltpu.make_async_remote_copy(
-            src_ref=dst.at[peer],
-            dst_ref=dst.at[peer],
-            send_sem=send_sem.at[x_mate, peer],
-            recv_sem=recv_sem.at[x, peer],
-            device_id=(me_s, mate),
-            device_id_type=MESH,
-        )
-
-    def pass_weight(x, x_mate, src, dst):
-        def fn(peer):
-            wait_from(x, peer, src, dst.at[peer], (me_s, peer))
-            mate_copy(x, x_mate, peer, dst).start()
-
-        over_x(fn)
-
-    def wait_weight(x, src, dst):
-        wait_from(x, mate, src, dst.at[mate], (me_s, mate))
-
-        def fn(peer):
-            other = peer + 1 - 2 * core
-            wait_from(x, other, src, dst.at[other], (me_s, mate))
-
-        over_x(fn)
-
-    def sent_weight(x, x_mate, src, dst):
-        over_x(lambda peer: ch_copy(x, peer, src, dst.at[me_c]).wait_send())
-        ch_copy(x, mate, src, dst.at[me_c]).wait_send()
-        over_x(lambda peer: mate_copy(x, x_mate, peer, dst).wait_send())
-
-    start_weight(X_WGATE, wg_own, wg_all)
-    start_weight(X_WOUT, w_out, wo_all)
+    def pass_weight(x, x_mate, dst):
+        arrived(x, dst.at[pl.ds(0, SIDE - 1)])
+        over_x(lambda p: copy_to(x_mate, (me_s, mate), dst.at[p], dst.at[p]).start())
+
+    def wait_weight(x_mate, dst):
+        arrived(x_mate, dst.at[pl.ds(0, SIDE)])
+
+    def sent_weight(x, x_mate, dst):
+        sent(x, dst.at[pl.ds(0, SIDE)])
+        sent(x_mate, dst.at[pl.ds(0, SIDE - 1)])
+
+    start_weight(X_WGATE, X_WGATE_MATE, wg_own, wg_all)
+    start_weight(X_WOUT, X_WOUT_MATE, w_out, wo_all)
 
     cat_copy.wait()
 
@@ -336,7 +303,7 @@
     lax.fori_loop(0, ITEMS // 256, turn, 0)
     cat_t[FULL : FULL + 16, :] = jnp.broadcast_to(cnt[...].astype(F32), (16, ITEMS)).astype(BF16)
 
-    wait_seq(X_CONV, lambda p: msg1.at[p], rcv1)
+    wait_seq(X_CONV, rcv1)
     rf[...] = rcv1[...].astype(F32)
     xpad[0:16, :] = jnp.zeros((16, LANE), F32)
     later = iota((LANE, LANE), 1) >= iota((LANE, LANE), 0)
@@ -399,11 +366,12 @@
 
     def chunk_copy(h, peer):
         span = pl.ds(2 * h, 2)
-        return ch_copy(X_ROWS + h, peer, rows_send.at[span, peer], rows_all.at[span, me_c])
+        src, dst = rows_send.at[span, peer], rows_all.at[span, me_c]
+        return copy_to(X_ROWS + h, (me_s, peer), src, dst)
 
     def target_copy(peer):
-        x = X_ROWS + CHUNKS - 1
-        return ch_copy(x, peer, rows_send.at[GROUPS, peer], rows_all.at[GROUPS, me_c])
+        src, dst = rows_send.at[GROUPS, peer], rows_all.at[GROUPS, me_c]
+        return copy_to(X_ROWS + CHUNKS - 1, (me_s, peer), src, dst)
 
     def fetch(first, last):
         def step(h, carry):
@@ -418,38 +386,19 @@
         keep(dot(cat_t[...], picked(GROUPS)), LANE, GROUPS)
         over(C, me_c, lambda peer: target_copy(peer).start())
 
-    def wait_rows():
+    def each_chunk(fn):
         def step(h, carry):
-            span = pl.ds(2 * h, 2)
-
-            def fn(peer):
-                src, dst = rows_send.at[span, peer], rows_all.at[span, peer]
-                wait_from(X_ROWS + h, peer, src, dst, (me_s, peer))
-
-            over(C, me_c, fn)
+            fn(X_ROWS + h, rows_all.at[pl.ds(2 * h, 2), pl.ds(0, C - 1)])
             return carry
 
         lax.fori_loop(0, CHUNKS - 1, step, 0)
-
-        def last(peer):
-            src, dst = rows_send.at[GROUPS, peer], rows_all.at[GROUPS, peer]
-            wait_from(X_ROWS + CHUNKS - 1, peer, src, dst, (me_s, peer))
-
-        over(C, me_c, last)
-
-    def sent_rows():
-        def step(h, carry):
-            over(C, me_c, lambda peer: chunk_copy(h, peer).wait_send())
-            return carry
-
-        lax.fori_loop(0, CHUNKS - 1, step, 0)
-        over(C, me_c, lambda peer: target_copy(peer).wait_send())
+        fn(X_ROWS + CHUNKS - 1, rows_all.at[GROUPS, pl.ds(0, C - 1)])
 
     fetch(0, 4)
-    pass_weight(X_WGATE, X_WGATE_MATE, wg_own, wg_all)
-    wait_ch(X_SIG, lambda p: sig_send.at[p], sig_all)
-
-    wait_seq(X_BACK, lambda p: msg2.at[p], rcv2)
+    pass_weight(X_WGATE, X_WGATE_MATE, wg_all)
+    wait_ch(X_SIG, sig_all)
+
+    wait_seq(X_BACK, rcv2)
     rf[...] = rcv2[...].astype(F32)
     msgf[...] = rf[...].reshape(S * 32, LANE)
     diag = iota((CH, CH), 0) == iota((CH, CH), 1)
@@ -461,14 +410,14 @@
         mix_send[q] = (conv + gain_col * sig_send[q].astype(F32)).astype(BF16)
     start_ch(X_MIX, lambda p: mix_send.at[p], mix_all)
     mix_all[me_c] = mix_send[me_c]
-    pass_weight(X_WOUT, X_WOUT_MATE, w_out, wo_all)
-
-    wait_weight(X_WGATE, wg_own, wg_all)
+    pass_weight(X_WOUT, X_WOUT_MATE, wo_all)
+
+    wait_weight(X_WGATE_MATE, wg_all)
     gate_t[...] = dot(wg_all[...].reshape(FULL, FULL), sig_all[...].reshape(FULL, LANE))
     fetch(4, 6)
-    wait_weight(X_WOUT, w_out, wo_all)
+    wait_weight(X_WOUT_MATE, wo_all)
     wo_t[...] = wo_all[...].reshape(FULL, FULL).T
-    wait_ch(X_MIX, lambda p: mix_send.at[p], mix_all)
+    wait_ch(X_MIX, mix_all)
     mix = mix_all[...].reshape(FULL, LANE).astype(F32) * gate_t[...]
     lo_send[...] = dot(wo_t[...], mix.astype(BF16)).astype(BF16).reshape(C, CH, LANE)
     start_ch(X_OUT, lambda p: lo_send.at[p], lo_all)
@@ -480,55 +429,47 @@
     where_in = ((pos_in >> 7) * 4 + (tok_pos & 3)) * LANE + (pos_in & 127)
     pick = onehot(iota((TOK, LANE), 0) == where_in)
 
-    wait_ch(X_OUT, lambda p: lo_send.at[p], lo_all)
+    wait_ch(X_OUT, lo_all)
     lo_t = jnp.concatenate([lo_all[q] for q in range(8)], axis=1)
     q_own[...] = dot(lo_t, pick).astype(BF16)
 
     me_z, me_y = me_s // SIDE, lax.rem(me_s, SIDE)
     layers = S // SIDE
 
-    def block_to(x, slot, peer, src, block):
-        return pltpu.make_async_remote_copy(
-            src_ref=src,
-            dst_ref=q_all.at[block],
-            send_sem=send_sem.at[x, slot],
-            recv_sem=recv_sem.at[X_QUERY, block],
-            device_id=(peer, me_c),
-            device_id_type=MESH,
-        )
-
     def along_z(fn):
         def step(d, carry):
-            fn(lax.rem(me_z + d, layers) * SIDE + me_y)
+            fn(lax.rem(me_z + d, layers))
             return carry
 
         lax.fori_loop(1, layers, step, 0)
 
-    def along_y(block, src, fn):
+    def along_y(block, src):
         def step(d, carry):
             peer = me_z * SIDE + lax.rem(me_y + d, SIDE)
-            fn(block_to(X_FORWARD, d * layers + block // SIDE, peer, src, block))
+            copy_to(X_FORWARD, (peer, me_c), src, q_all.at[block]).start()
             return carry
 
         lax.fori_loop(1, SIDE, step, 0)
 
-    def take_block(block):
-        wait_from(X_QUERY, block, q_own, q_all.at[block], (block, me_c))
-
-    along_z(lambda peer: block_to(X_QUERY, peer, peer, q_own, me_s).start())
-    along_y(me_s, q_own, lambda copy: copy.start())
+    along_z(
+        lambda z: copy_to(
+            X_QUERY, (z * SIDE + me_y, me_c), q_own, q_all.at[me_s], X_LAYER + me_z
+        ).start()
+    )
+    along_y(me_s, q_own)
     q_all[me_s] = q_own[...]
     for q in range(8):
         out_ref[q % 4, :, (q // 4) * LANE : (q // 4 + 1) * LANE] = lo_all[q]
 
-    def go_on(block):
-        take_block(block)
-        along_y(block, q_all.at[block], lambda copy: copy.start())
+    def go_on(z):
+        block = z * SIDE + me_y
+        arrived(X_LAYER + z, q_own)
+        along_y(block, q_all.at[block])
 
     along_z(go_on)
     fetch_targets()
 
-    wait_ch(X_TABLE, lambda p: tab_own, tab_all)
+    wait_ch(X_TABLE, tab_all)
     pair_ids = iota((2 * LANE, LANE), 0)
 
     def slots(g, carry):
@@ -555,7 +496,7 @@
     for g in range(GROUPS + 1):
         slot_pos[g] = onehot(columns[:, g : g + 1] == pos_ids)
 
-    wait_rows()
+    each_chunk(arrived)
     tgt_rows = []
     for lane0 in TGT_LANES:
         rows = jnp.zeros((CH, LANE), F32)
@@ -565,17 +506,7 @@
         tgt_rows.append(rows)
     part[...] = jnp.zeros_like(part)
 
-    def rest_of_blocks(d, carry):
-        y = lax.rem(me_y + d, SIDE)
-
-        def step(z, inside):
-            take_block(z * SIDE + y)
-            return inside
-
-        lax.fori_loop(0, layers, step, 0)
-        return carry
-
-    lax.fori_loop(1, SIDE, rest_of_blocks, 0)
+    arrived(X_FORWARD, q_all.at[pl.ds(0, S - layers)])
 
     def pair(g, carry):
         both = jnp.concatenate([q_all[2 * g], q_all[2 * g + 1]], axis=1)
@@ -603,7 +534,7 @@
         part[c, 24 + GROUPS : 25 + GROUPS, :] = tgt_part[c][1]
     start_ch(X_PART, lambda p: part.at[p], part_all)
     part_all[me_c] = part[me_c]
-    wait_ch(X_PART, lambda p: part.at[p], part_all)
+    wait_ch(X_PART, part_all)
     whole = jnp.sum(part_all[...], axis=0)
     query_scale = lax.rsqrt(whole[24:48] / FULL + EPSILON)
     logit = whole[0:24] * query_scale * row_scale[...] - row_log[...]
@@ -625,30 +556,29 @@
         sums[2 * g + 1, 0:1, :] = found[32 + g : 33 + g] + found[48 + g : 49 + g]
     start_seq(X_SUMS, lambda p: sums.at[p], sums_all)
     sums_all[me_s] = sums[me_s]
-    wait_seq(X_SUMS, lambda p: sums.at[p], sums_all)
+    wait_seq(X_SUMS, sums_all)
     fin[...] = jnp.sum(sums_all[...], axis=0)
     start_ch(X_FIN, lambda p: fin, fin_all)
     fin_all[me_c] = fin[...]
-    wait_ch(X_FIN, lambda p: fin, fin_all)
+    wait_ch(X_FIN, fin_all)
     last = jnp.sum(fin_all[...], axis=0)
     target_logit = last[1:2]
     loss_ref[...] = jnp.log(jnp.exp(target_logit) + last[0:1]) - target_logit
 
-    sent_seq(X_CONV, lambda p: msg1.at[p], rcv1)
-    sent_seq(X_BACK, lambda p: msg2.at[p], rcv2)
-    along_z(lambda peer: block_to(X_QUERY, peer, peer, q_own, me_s).wait_send())
-    along_y(me_s, q_own, lambda copy: copy.wait_send())
-    along_z(lambda block: along_y(block, q_all.at[block], lambda copy: copy.wait_send()))
-    sent_seq(X_SUMS, lambda p: sums.at[p], sums_all)
-    sent_ch(X_SIG, lambda p: sig_send.at[p], sig_all)
-    sent_weight(X_WGATE, X_WGATE_MATE, wg_own, wg_all)
-    sent_weight(X_WOUT, X_WOUT_MATE, w_out, wo_all)
-    sent_ch(X_TABLE, lambda p: tab_own, tab_all)
-    sent_rows()
-    sent_ch(X_MIX, lambda p: mix_send.at[p], mix_all)
-    sent_ch(X_OUT, lambda p: lo_send.at[p], lo_all)
-    sent_ch(X_PART, lambda p: part.at[p], part_all)
-    sent_ch(X_FIN, lambda p: fin, fin_all)
+    sent_seq(X_CONV, rcv1)
+    sent_seq(X_BACK, rcv2)
+    sent(X_QUERY, q_all.at[pl.ds(0, layers - 1)])
+    sent(X_FORWARD, q_all.at[pl.ds(0, S - layers)])
+    sent_seq(X_SUMS, sums_all)
+    sent_ch(X_SIG, sig_all)
+    sent_weight(X_WGATE, X_WGATE_MATE, wg_all)
+    sent_weight(X_WOUT, X_WOUT_MATE, wo_all)
+    sent_ch(X_TABLE, tab_all)
+    each_chunk(sent)
+    sent_ch(X_MIX, mix_all)
+    sent_ch(X_OUT, lo_all)
+    sent_ch(X_PART, part_all)
+    sent_ch(X_FIN, fin_all)
 
 
 def per_device(
@@ -721,7 +651,7 @@
         in_specs=[vmem] * 5 + [pl.BlockSpec(memory_space=pl.ANY)] + [vmem] * 6,
         out_specs=(vmem, vmem),
         scratch_shapes=[pltpu.VMEM(shape, kind) for shape, kind in scratch]
-        + [pltpu.SemaphoreType.DMA((EXCHANGES, S))] * 2
+        + [pltpu.SemaphoreType.DMA((EXCHANGES,))] * 2
         + [pltpu.SemaphoreType.DMA(())],
         compiler_params=pltpu.CompilerParams(
             collective_id=0, has_side_effects=True, vmem_limit_bytes=60 * 1024 * 1024

time: 116 us -> 100 us (0.86)
  Pallas kernels: 113 us -> 96.9 us
    pallas_call x1, Pallas kernels: 113 us -> 96.9 us  [per_device(): pl.pallas_call(body, out_shape=(jax.ShapeDtypeStruct((4, CH, 256), BF16),...]
where the time goes in v3:
time: 100 us
  Pallas kernels  96.9 us (97%)
  local copies, waits for them, and re-layouts  2.75 us (3%)
    pallas_call x1, Pallas kernels, per_device(): pl.pallas_call(body, out_shape=(jax.ShapeDtypeStruct((4, CH, 256), BF16),...  96.9 us
    unnamed x2, local copies, waits for them, and re-layouts  2.75 us

profile of v3, /device:TPU:1, one launch (start us, length us, event | category | flops | bytes accessed | tf_op | source)
XLA Modules:
  0.0 100.3 jit_solution(8258513512219222523)
XLA Ops:
  0.6 96.9 %shard_map.131 = (bf16[4,96,256]{2,1,0:T(8,128)(2,1)}, f32[1,128]{1,0:T(1,128)}) custom-call(bf16[4,96,256]{2,1,0:T(8,128)(2,1)} %bitcast.13, f32[96,256]{1,0:T(8,128)} %bitcast.15, f32[1,96]{1,0:T(1,128)} %bitcast.19, bf16[96,768]{1,0:T(8,128)(2,1)} %bitcast.14, bf16[96,768]{1,0:T(8,128)(2,1)} %w_out.1, bf16[2048,768]{1,0:T(8,128)(2,1)} %cat_hbm.1, ...), custom_call_target="tpu_custom_call" | custom-call | flops 20000000000 | bytes 5000000 | tf_op jit(solution)/shard_map/pallas_call | solution.py:645
  97.6 1.6 %copy.16 = bf16[256,4,96]{0,2,1:T(8,128)(2,1)} copy(bf16[256,4,96]{0,2,1:T(8,128)(2,1)} %bitcast.12) | data formatting | bytes 393216
  99.2 1.1 %copy.17 = f32[128]{0:T(128)} copy(f32[128]{0:T(128)} %bitcast.23) | data formatting | bytes 1024

commit v4 on v3

--- a/solution.py
+++ b/solution.py
@@ -28,6 +28,7 @@
     X_BACK,
     X_QUERY,
     X_FORWARD,
+    X_ACROSS,
     X_SUMS,
     X_SIG,
     X_WGATE,
@@ -35,14 +36,17 @@
     X_WGATE_MATE,
     X_WOUT_MATE,
     X_TABLE,
+    X_TABLE_Y,
     X_MIX,
     X_OUT,
     X_PART,
+    X_PART_Y,
     X_FIN,
     X_ROWS,
-) = range(16)
-X_LAYER = X_ROWS + GROUPS // 2 + 1
-CHUNKS = GROUPS // 2 + 1
+) = range(19)
+X_LAYER = X_ROWS + GROUPS // 2 + 2
+CHUNKS = GROUPS // 2
+HALF = GROUPS // 2
 EXCHANGES = X_LAYER + 8
 SIDE = 4
 TGT_LANES = (0, 16, 64, 80)
@@ -106,6 +110,7 @@
     lo_send,
     lo_all,
     q_own,
+    q_stage,
     q_all,
     ohs,
     inner,
@@ -135,6 +140,17 @@
 ):
     me_s = lax.axis_index("seq")
     me_c = lax.axis_index("ch")
+    me_z, me_y = me_s // SIDE, lax.rem(me_s, SIDE)
+    me_x, core = me_c // 2, lax.rem(me_c, 2)
+    me_v = me_y * 2 + core
+    layers = S // SIDE
+
+    def beside(y, x):
+        return (me_z * SIDE + y, x * 2 + core)
+
+    def split_peer(along_x, p):
+        seq = jnp.where(along_x, me_s, me_z * SIDE + p // 2)
+        return (seq, jnp.where(along_x, p, me_x * 2 + lax.rem(p, 2)))
 
     def copy_to(x, device, src, dst, x_recv=None):
         return pltpu.make_async_remote_copy(
@@ -187,6 +203,18 @@
 
     over(S, me_s, greet_seq)
     over(C, me_c, greet_ch)
+    for y in range(SIDE):
+
+        @pl.when(me_y != y)
+        def _():
+            other = (me_z * SIDE + y, me_x * 2 + 1 - core)
+            pl.semaphore_signal(barrier, inc=1, device_id=other, device_id_type=MESH)
+
+        @pl.when((me_y != y) | (me_x != me_y))
+        def _():
+            pl.semaphore_signal(barrier, inc=1, device_id=beside(y, me_y), device_id_type=MESH)
+
+    on_diagonal = me_x == me_y
 
     cat_copy = pltpu.make_async_copy(cat_hbm, cat, cat_sem)
     cat_copy.start()
@@ -257,14 +285,14 @@
     msgf[pl.ds(31, S, stride=32), :] = entry_low
     msg1[...] = msgf[...].reshape(S, 32, LANE).astype(BF16)
 
-    pl.semaphore_wait(barrier, S - 1 + C - 1)
+    extra = SIDE - 1 + SIDE - jnp.where(on_diagonal, 1, 0)
+    pl.semaphore_wait(barrier, S - 1 + C - 1 + extra)
 
     start_seq(X_CONV, lambda p: msg1.at[p], rcv1)
     rcv1[me_s] = msg1[me_s]
     start_ch(X_SIG, lambda p: sig_send.at[p], sig_all)
     sig_all[me_c] = sig_send[me_c]
 
-    core = lax.rem(me_c, 2)
     mate = me_c + 1 - 2 * core
 
     def over_x(fn):
@@ -342,8 +370,14 @@
     tab_own[GROUPS : GROUPS + 1, :] = jnp.max(
         jnp.where(first_half, odd_half, even_half), axis=0, keepdims=True
     )
-    start_ch(X_TABLE, lambda p: tab_own, tab_all)
-    tab_all[me_c] = tab_own[...]
+    start_ch(X_TABLE, lambda p: tab_own, tab_all.at[0])
+    tab_all[0, me_c] = tab_own[...]
+
+    def table_along_y(p):
+        copy_to(X_TABLE_Y, split_peer(False, p), tab_own, tab_all.at[1, me_v]).start()
+
+    over(C, me_v, table_along_y)
+    tab_all[1, me_v] = tab_own[...]
     row_scale[...] = jnp.zeros_like(row_scale)
     row_log[...] = jnp.zeros_like(row_log)
     item_ids = iota((ITEMS, LANE), 0)
@@ -356,7 +390,9 @@
             lanes = slice(i * LANE, (i + 1) * LANE)
             for c in range(C):
                 rows_send[group0 + i, c] = found[c * CH : (c + 1) * CH, lanes].astype(BF16)
-            rows_all[group0 + i, me_c] = rows_send[group0 + i, me_c]
+            if width > LANE:
+                mine = jnp.where(group0 < HALF, me_c, me_v)
+                rows_all[group0 + i, mine] = rows_send[group0 + i, mine]
         square = jnp.sum(found[0:FULL] * found[0:FULL], axis=0, keepdims=True)
         scale = lax.rsqrt(square / FULL + EPSILON) / (FULL * SOFTMAX_TEMP)
         logs = jnp.log(jnp.maximum(found[FULL : FULL + 1], 1.0))
@@ -364,35 +400,40 @@
             row_scale[pl.ds(group0 + i, 1), :] = scale[:, i * LANE : (i + 1) * LANE]
             row_log[pl.ds(group0 + i, 1), :] = logs[:, i * LANE : (i + 1) * LANE]
 
-    def chunk_copy(h, peer):
-        span = pl.ds(2 * h, 2)
-        src, dst = rows_send.at[span, peer], rows_all.at[span, me_c]
-        return copy_to(X_ROWS + h, (me_s, peer), src, dst)
-
-    def target_copy(peer):
-        src, dst = rows_send.at[GROUPS, peer], rows_all.at[GROUPS, me_c]
-        return copy_to(X_ROWS + CHUNKS - 1, (me_s, peer), src, dst)
+    def send_rows(x, span, to, along_x):
+        mine = jnp.where(along_x, me_c, me_v)
+
+        def fn(p):
+            src, dst = rows_send.at[span, p], rows_all.at[to, mine]
+            copy_to(x, split_peer(along_x, p), src, dst).start()
+
+        over(C, mine, fn)
 
     def fetch(first, last):
-        def step(h, carry):
+        def step(i, carry):
+            h = lax.rem(i, 2) * (CHUNKS // 2) + i // 2
             hot = jnp.concatenate([picked(2 * h), picked(2 * h + 1)], axis=1)
             keep(dot(cat_t[...], hot), 256, 2 * h)
-            over(C, me_c, lambda peer: chunk_copy(h, peer).start())
+            send_rows(X_ROWS + h, pl.ds(2 * h, 2), pl.ds(2 * h, 2), h < CHUNKS // 2)
             return carry
 
         lax.fori_loop(first, last, step, 0)
 
     def fetch_targets():
         keep(dot(cat_t[...], picked(GROUPS)), LANE, GROUPS)
-        over(C, me_c, lambda peer: target_copy(peer).start())
+        rows_all[GROUPS, me_c] = rows_send[GROUPS, me_c]
+        rows_all[GROUPS + 1, me_v] = rows_send[GROUPS, me_v]
+        send_rows(X_ROWS + CHUNKS, GROUPS, GROUPS, True)
+        send_rows(X_ROWS + CHUNKS + 1, GROUPS, GROUPS + 1, False)
 
     def each_chunk(fn):
         def step(h, carry):
             fn(X_ROWS + h, rows_all.at[pl.ds(2 * h, 2), pl.ds(0, C - 1)])
             return carry
 
-        lax.fori_loop(0, CHUNKS - 1, step, 0)
-        fn(X_ROWS + CHUNKS - 1, rows_all.at[GROUPS, pl.ds(0, C - 1)])
+        lax.fori_loop(0, CHUNKS, step, 0)
+        for i in range(2):
+            fn(X_ROWS + CHUNKS + i, rows_all.at[GROUPS + i, pl.ds(0, C - 1)])
 
     fetch(0, 4)
     pass_weight(X_WGATE, X_WGATE_MATE, wg_all)
@@ -433,9 +474,6 @@
     lo_t = jnp.concatenate([lo_all[q] for q in range(8)], axis=1)
     q_own[...] = dot(lo_t, pick).astype(BF16)
 
-    me_z, me_y = me_s // SIDE, lax.rem(me_s, SIDE)
-    layers = S // SIDE
-
     def along_z(fn):
         def step(d, carry):
             fn(lax.rem(me_z + d, layers))
@@ -443,38 +481,65 @@
 
         lax.fori_loop(1, layers, step, 0)
 
-    def along_y(block, src):
-        def step(d, carry):
-            peer = me_z * SIDE + lax.rem(me_y + d, SIDE)
-            copy_to(X_FORWARD, (peer, me_c), src, q_all.at[block]).start()
+    def go_on(z):
+        block = z * SIDE + me_y
+        first = z < layers // 2
+        src = q_stage.at[z]
+
+        def step(j, carry):
+            y = jnp.where(first, j, me_x)
+            x = jnp.where(first, me_x, j)
+            here = (y == me_y) & (x == me_x)
+
+            @pl.when(jnp.logical_not(here))
+            def _():
+                way = jnp.where(first, X_FORWARD, X_ACROSS)
+                copy_to(way, beside(y, x), src, q_all.at[block]).start()
+
+            @pl.when(here)
+            def _():
+                q_all[block] = q_stage[z]
+
             return carry
 
-        lax.fori_loop(1, SIDE, step, 0)
-
+        lax.fori_loop(0, SIDE, step, 0)
+
+    q_stage[me_z] = q_own[...]
     along_z(
         lambda z: copy_to(
-            X_QUERY, (z * SIDE + me_y, me_c), q_own, q_all.at[me_s], X_LAYER + me_z
+            X_QUERY, (z * SIDE + me_y, me_c), q_own, q_stage.at[me_z], X_LAYER + me_z
         ).start()
     )
-    along_y(me_s, q_own)
-    q_all[me_s] = q_own[...]
+    go_on(me_z)
     for q in range(8):
         out_ref[q % 4, :, (q // 4) * LANE : (q // 4 + 1) * LANE] = lo_all[q]
 
-    def go_on(z):
-        block = z * SIDE + me_y
+    def take_layer(z):
         arrived(X_LAYER + z, q_own)
-        along_y(block, q_all.at[block])
-
-    along_z(go_on)
+        go_on(z)
+
+    along_z(take_layer)
+
+    def each_way(fn):
+        fn(X_FORWARD, q_all.at[pl.ds(0, 12)])
+
+        @pl.when(on_diagonal)
+        def _():
+            fn(X_ACROSS, q_all.at[pl.ds(0, 12)])
+
+        @pl.when(jnp.logical_not(on_diagonal))
+        def _():
+            fn(X_ACROSS, q_all.at[pl.ds(0, 16)])
+
     fetch_targets()
 
-    wait_ch(X_TABLE, tab_all)
+    wait_ch(X_TABLE, tab_all.at[0])
+    wait_ch(X_TABLE_Y, tab_all.at[1])
     pair_ids = iota((2 * LANE, LANE), 0)
 
     def slots(g, carry):
         for c in range(C):
-            entry = tab_all[c, pl.ds(g, 1), :]
+            entry = tab_all[g // HALF, c, pl.ds(g, 1), :]
             target = jnp.where(entry < 0, -1, (entry & 127) + jnp.where(lane_row < NEG, 0, LANE))
             ohp[g, :, c * LANE : (c + 1) * LANE] = onehot(pair_ids == target)
         return carry
@@ -485,7 +550,8 @@
     for o, lane0 in enumerate(TGT_LANES):
         entry = jnp.full((1, LANE), -1, I32)
         for c in range(C):
-            turned = pltpu.roll(tab_all[c, GROUPS : GROUPS + 1, :], (16 * c - lane0) % LANE, 1)
+            listed = tab_all[o % 2, c, GROUPS : GROUPS + 1, :]
+            turned = pltpu.roll(listed, (16 * c - lane0) % LANE, 1)
             entry = jnp.where(part_of == c, turned, entry)
         target = jnp.where(entry < 0, -1, ((lane_row & 15) >> 1) * LANE + (entry & 127))
         oht[o] = onehot(wide_ids == target)
@@ -498,15 +564,16 @@
 
     each_chunk(arrived)
     tgt_rows = []
-    for lane0 in TGT_LANES:
+    for o, lane0 in enumerate(TGT_LANES):
         rows = jnp.zeros((CH, LANE), F32)
         for c in range(C):
-            turned = pltpu.roll(rows_all[GROUPS, c].astype(F32), (16 * c - lane0) % LANE, 1)
+            there = rows_all[GROUPS + o % 2, c].astype(F32)
+            turned = pltpu.roll(there, (16 * c - lane0) % LANE, 1)
             rows = jnp.where(part_of == c, turned, rows)
         tgt_rows.append(rows)
     part[...] = jnp.zeros_like(part)
 
-    arrived(X_FORWARD, q_all.at[pl.ds(0, S - layers)])
+    each_way(arrived)
 
     def pair(g, carry):
         both = jnp.concatenate([q_all[2 * g], q_all[2 * g + 1]], axis=1)
@@ -514,12 +581,14 @@
         for c in range(C):
             one = query[:, c * LANE : (c + 1) * LANE]
             rows = rows_all[g, c].astype(F32)
-            part[c, pl.ds(g, 1), :] = jnp.sum(one * rows, axis=0, keepdims=True)
-            part[c, pl.ds(24 + g, 1), :] = jnp.sum(one * one, axis=0, keepdims=True)
+            place = pl.ds(lax.rem(g, HALF), 1)
+            square_place = pl.ds(16 + lax.rem(g, HALF), 1)
+            part[g // HALF, c, place, :] = jnp.sum(one * rows, axis=0, keepdims=True)
+            part[g // HALF, c, square_place, :] = jnp.sum(one * one, axis=0, keepdims=True)
         return carry
 
     lax.fori_loop(0, GROUPS, pair, 0, unroll=2)
-    tgt_part = [[jnp.zeros((1, LANE), F32) for _ in range(2)] for _ in range(C)]
+    tgt_part = [[[jnp.zeros((1, LANE), F32)] * 2 for _ in range(C)] for _ in range(2)]
     for o, lane0 in enumerate(TGT_LANES):
         wide = jnp.concatenate([q_all[b] for b in TGT_BLOCKS[o]], axis=1)
         one = dot(wide, oht[o])
@@ -528,14 +597,30 @@
             for c in range(C):
                 turned = pltpu.roll(both, (lane0 - 16 * c) % LANE, 1)
                 ours = (lane_row >= lane0) & (lane_row < lane0 + 16)
-                tgt_part[c][i] = jnp.where(ours, turned, tgt_part[c][i])
-    for c in range(C):
-        part[c, GROUPS : GROUPS + 1, :] = tgt_part[c][0]
-        part[c, 24 + GROUPS : 25 + GROUPS, :] = tgt_part[c][1]
-    start_ch(X_PART, lambda p: part.at[p], part_all)
-    part_all[me_c] = part[me_c]
-    wait_ch(X_PART, part_all)
-    whole = jnp.sum(part_all[...], axis=0)
+                tgt_part[o % 2][c][i] = jnp.where(ours, turned, tgt_part[o % 2][c][i])
+    for way in range(2):
+        for c in range(C):
+            part[way, c, HALF : HALF + 1, :] = tgt_part[way][c][0]
+            part[way, c, 16 + HALF : 17 + HALF, :] = tgt_part[way][c][1]
+    start_ch(X_PART, lambda p: part.at[0, p], part_all.at[0])
+    part_all[0, me_c] = part[0, me_c]
+
+    def part_along_y(p):
+        copy_to(X_PART_Y, split_peer(False, p), part.at[1, p], part_all.at[1, me_v]).start()
+
+    over(C, me_v, part_along_y)
+    part_all[1, me_v] = part[1, me_v]
+    wait_ch(X_PART, part_all.at[0])
+    wait_ch(X_PART_Y, part_all.at[1])
+    by_x, by_y = jnp.sum(part_all[0], axis=0), jnp.sum(part_all[1], axis=0)
+    whole = jnp.concatenate(
+        [
+            piece
+            for i in (0, 16)
+            for piece in (by_x[i : i + 8], by_y[i : i + 8], by_x[i + 8 : i + 16] + by_y[i + 8 : i + 16])
+        ],
+        axis=0,
+    )
     query_scale = lax.rsqrt(whole[24:48] / FULL + EPSILON)
     logit = whole[0:24] * query_scale * row_scale[...] - row_log[...]
     filled = tab_own[...] >= 0
@@ -568,16 +653,18 @@
     sent_seq(X_CONV, rcv1)
     sent_seq(X_BACK, rcv2)
     sent(X_QUERY, q_all.at[pl.ds(0, layers - 1)])
-    sent(X_FORWARD, q_all.at[pl.ds(0, S - layers)])
+    each_way(sent)
     sent_seq(X_SUMS, sums_all)
     sent_ch(X_SIG, sig_all)
     sent_weight(X_WGATE, X_WGATE_MATE, wg_all)
     sent_weight(X_WOUT, X_WOUT_MATE, wo_all)
-    sent_ch(X_TABLE, tab_all)
+    sent_ch(X_TABLE, tab_all.at[0])
+    sent_ch(X_TABLE_Y, tab_all.at[1])
     each_chunk(sent)
     sent_ch(X_MIX, mix_all)
     sent_ch(X_OUT, lo_all)
-    sent_ch(X_PART, part_all)
+    sent_ch(X_PART, part_all.at[0])
+    sent_ch(X_PART_Y, part_all.at[1])
     sent_ch(X_FIN, fin_all)
 
 
@@ -618,6 +705,7 @@
         ((C, CH, LANE), BF16),
         ((C, CH, LANE), BF16),
         ((CH, LANE), BF16),
+        ((S // SIDE, CH, LANE), BF16),
         ((S, CH, LANE), BF16),
         ((64 * S, LANE), BF16),
         ((64 * S, LANE), F32),
@@ -625,18 +713,18 @@
         ((LANE, 64 * LANE), BF16),
         ((LANE, 64 * LANE), BF16),
         ((24, LANE), I32),
-        ((C, 24, LANE), I32),
+        ((2, C, 24, LANE), I32),
         ((LANE, LANE), F32),
         ((FULL + 16, ITEMS), BF16),
         ((GROUPS + 1, C, CH, LANE), BF16),
-        ((GROUPS + 1, C, CH, LANE), BF16),
+        ((GROUPS + 2, C, CH, LANE), BF16),
         ((24, LANE), F32),
         ((24, LANE), F32),
         ((GROUPS, 2 * LANE, C * LANE), BF16),
         ((len(TGT_LANES), 8 * LANE, LANE), BF16),
         ((GROUPS + 1, LANE, LANE), BF16),
-        ((C, 48, LANE), F32),
-        ((C, 48, LANE), F32),
+        ((2, C, 32, LANE), F32),
+        ((2, C, 32, LANE), F32),
         ((S, 8, LANE), F32),
         ((S, 8, LANE), F32),
         ((8, LANE), F32),

time: 100 us -> 90.4 us (0.904)
  Pallas kernels: 96.9 us -> 86.9 us
    pallas_call x1, Pallas kernels: 96.9 us -> 86.9 us  [per_device(): pl.pallas_call(body, out_shape=(jax.ShapeDtypeStruct((4, CH, 256), BF16),...]
where the time goes in v4:
time: 90.4 us; the launch traced here: 90.3 us
  Pallas kernels  86.9 us (96%)
  local copies, waits for them, and re-layouts  2.75 us (3%)
    pallas_call x1, Pallas kernels, per_device(): pl.pallas_call(body, out_shape=(jax.ShapeDtypeStruct((4, CH, 256), BF16),...  86.9 us
    unnamed x2, local copies, waits for them, and re-layouts  2.75 us

profile of v4, /device:TPU:1, one launch (start us, length us, event | category | flops | bytes accessed | tf_op | source)
XLA Modules:
  0.0 90.3 jit_solution(2002171684841138825)
XLA Ops:
  0.6 86.9 %shard_map.131 = (bf16[4,96,256]{2,1,0:T(8,128)(2,1)}, f32[1,128]{1,0:T(1,128)}) custom-call(bf16[4,96,256]{2,1,0:T(8,128)(2,1)} %bitcast.13, f32[96,256]{1,0:T(8,128)} %bitcast.15, f32[1,96]{1,0:T(1,128)} %bitcast.19, bf16[96,768]{1,0:T(8,128)(2,1)} %bitcast.14, bf16[96,768]{1,0:T(8,128)(2,1)} %w_out.1, bf16[2048,768]{1,0:T(8,128)(2,1)} %cat_hbm.1, ...), custom_call_target="tpu_custom_call" | custom-call | flops 20000000000 | bytes 5000000 | tf_op jit(solution)/shard_map/pallas_call | solution.py:733
  87.5 1.6 %copy.16 = bf16[256,4,96]{0,2,1:T(8,128)(2,1)} copy(bf16[256,4,96]{0,2,1:T(8,128)(2,1)} %bitcast.12) | data formatting | bytes 393216
  89.1 1.1 %copy.17 = f32[128]{0:T(128)} copy(f32[128]{0:T(128)} %bitcast.23) | data formatting | bytes 1024

commit v5 on v4

--- a/solution.py
+++ b/solution.py
@@ -25,6 +25,7 @@
 
 (
     X_CONV,
+    X_REQ,
     X_BACK,
     X_QUERY,
     X_FORWARD,
@@ -43,11 +44,13 @@
     X_PART_Y,
     X_FIN,
     X_ROWS,
-) = range(19)
+) = range(20)
 X_LAYER = X_ROWS + GROUPS // 2 + 2
 CHUNKS = GROUPS // 2
+EARLY = 6
 HALF = GROUPS // 2
-EXCHANGES = X_LAYER + 8
+X_WAY = X_LAYER + 8
+EXCHANGES = X_WAY + 8
 SIDE = 4
 TGT_LANES = (0, 16, 64, 80)
 TGT_BLOCKS = tuple(tuple(range(first, first + 16, 2)) for first in (1, 17, 0, 16))
@@ -112,6 +115,8 @@
     q_own,
     q_stage,
     q_all,
+    req_msg,
+    req_all,
     ohs,
     inner,
     total,
@@ -219,58 +224,6 @@
     cat_copy = pltpu.make_async_copy(cat_hbm, cat, cat_sem)
     cat_copy.start()
 
-    upper = onehot(iota((LANE, LANE), 0) < iota((LANE, LANE), 1))
-    ones = jnp.ones((LANE, LANE), BF16)
-    owner_ids = iota((S, LANE), 0)
-
-    def own_onehot(owners):
-        mine = jnp.where((owners & 7) == me_c, owners >> 3, -1)
-        return jnp.where(owner_ids == mine, 1.0, 0.0)
-
-    def mark(m, carry):
-        ohs[pl.ds(pl.multiple_of(m * S, S), S), :] = own_onehot(nown[m]).astype(BF16)
-        return carry
-
-    lax.fori_loop(0, 64, mark, 0, unroll=4)
-    inner[...] = dot(ohs[...], upper)
-    total[...] = dot(ohs[...], ones)
-    key_ids = iota((LANE, LANE), 0).astype(F32)
-    lane_row = iota((1, LANE), 1)
-
-    def key_of(hot, rank, offset):
-        found = jnp.sum(hot * (rank + 1.0), axis=0, keepdims=True)
-        place = jnp.where(found > 0.5, found - 1.0 + offset, -1.0)
-        return jnp.where(key_ids == place, 1.0, 0.0).astype(BF16)
-
-    def value_of(hot, rows):
-        high = (rows >> 8).astype(F32)
-        low = (rows & 255).astype(F32)
-        pieces = [hot * high, hot * low, hot * lane_row.astype(F32), hot]
-        return jnp.concatenate(pieces, axis=0).astype(BF16)
-
-    odd = lax.rem(me_s, 2)
-    neg_offset = (odd * NEG).astype(F32)
-    tgt_offset = ((1 - odd) * NEG + me_s - odd).astype(F32)
-
-    def place(m, before):
-        rows = pl.ds(pl.multiple_of(m * S, S), S)
-        lanes = pl.ds(pl.multiple_of(m * LANE, LANE), LANE)
-        hot = ohs[rows, :].astype(F32)
-        keys[:, lanes] = key_of(hot, inner[rows, :] + before, neg_offset)
-        vals[:, lanes] = value_of(hot, nrow[pl.ds(m, 1), :])
-        return before + total[rows, :]
-
-    lax.fori_loop(0, 64, place, jnp.zeros((S, LANE), F32), unroll=4)
-    hot = own_onehot(town[...])
-    rank = dot(hot.astype(BF16), upper)
-    found = dot(vals[...], keys[...], 1, 1) + dot(
-        value_of(hot, trow[...]), key_of(hot, rank, tgt_offset), 1, 1
-    )
-    high, low, pos, filled = (found[i * S : (i + 1) * S].astype(I32) for i in range(4))
-    entry = (high * 256 + low) * LANE + pos
-    entry_high = jnp.where(filled > 0, (entry >> 9) - 256, 1024).astype(F32)
-    entry_low = jnp.where(filled > 0, (entry & 511) - 256, 0).astype(F32)
-
     for q in range(8):
         piece = sig[q % 4, :, (q // 4) * LANE : (q // 4 + 1) * LANE]
         sig_send[q] = piece
@@ -281,8 +234,8 @@
             msgf[pl.ds(24 + 2 * k + il, S, stride=32), :] = taps_t[
                 k * 32 : (k + 1) * 32, il * LANE : (il + 1) * LANE
             ]
-    msgf[pl.ds(30, S, stride=32), :] = entry_high
-    msgf[pl.ds(31, S, stride=32), :] = entry_low
+    for row in range(30, 32):
+        msgf[pl.ds(row, S, stride=32), :] = jnp.zeros((S, LANE), F32)
     msg1[...] = msgf[...].reshape(S, 32, LANE).astype(BF16)
 
     extra = SIDE - 1 + SIDE - jnp.where(on_diagonal, 1, 0)
@@ -321,15 +274,58 @@
     start_weight(X_WGATE, X_WGATE_MATE, wg_own, wg_all)
     start_weight(X_WOUT, X_WOUT_MATE, w_out, wo_all)
 
-    cat_copy.wait()
-
-    def turn(i, carry):
-        span = pl.ds(pl.multiple_of(i * 256, 256), 256)
-        cat_t[0:FULL, span] = cat[span, :].T
+    upper = onehot(iota((LANE, LANE), 0) < iota((LANE, LANE), 1))
+    ones = jnp.ones((LANE, LANE), BF16)
+    owner_ids = iota((S, LANE), 0)
+
+    def own_onehot(owners):
+        mine = jnp.where((owners & 7) == me_c, owners >> 3, -1)
+        return jnp.where(owner_ids == mine, 1.0, 0.0)
+
+    def mark(m, carry):
+        ohs[pl.ds(pl.multiple_of(m * S, S), S), :] = own_onehot(nown[m]).astype(BF16)
         return carry
 
-    lax.fori_loop(0, ITEMS // 256, turn, 0)
-    cat_t[FULL : FULL + 16, :] = jnp.broadcast_to(cnt[...].astype(F32), (16, ITEMS)).astype(BF16)
+    lax.fori_loop(0, 64, mark, 0, unroll=4)
+    inner[...] = dot(ohs[...], upper)
+    total[...] = dot(ohs[...], ones)
+    key_ids = iota((LANE, LANE), 0).astype(F32)
+    lane_row = iota((1, LANE), 1)
+
+    def key_of(hot, rank, offset):
+        found = jnp.sum(hot * (rank + 1.0), axis=0, keepdims=True)
+        place = jnp.where(found > 0.5, found - 1.0 + offset, -1.0)
+        return jnp.where(key_ids == place, 1.0, 0.0).astype(BF16)
+
+    def value_of(hot, rows):
+        high = (rows >> 8).astype(F32)
+        low = (rows & 255).astype(F32)
+        pieces = [hot * high, hot * low, hot * lane_row.astype(F32), hot]
+        return jnp.concatenate(pieces, axis=0).astype(BF16)
+
+    odd = lax.rem(me_s, 2)
+    neg_offset = (odd * NEG).astype(F32)
+    tgt_offset = ((1 - odd) * NEG + me_s - odd).astype(F32)
+
+    def place(m, before):
+        rows = pl.ds(pl.multiple_of(m * S, S), S)
+        lanes = pl.ds(pl.multiple_of(m * LANE, LANE), LANE)
+        hot = ohs[rows, :].astype(F32)
+        keys[:, lanes] = key_of(hot, inner[rows, :] + before, neg_offset)
+        vals[:, lanes] = value_of(hot, nrow[pl.ds(m, 1), :])
+        return before + total[rows, :]
+
+    lax.fori_loop(0, 64, place, jnp.zeros((S, LANE), F32), unroll=4)
+    hot = own_onehot(town[...])
+    rank = dot(hot.astype(BF16), upper)
+    found = dot(vals[...], keys[...], 1, 1) + dot(
+        value_of(hot, trow[...]), key_of(hot, rank, tgt_offset), 1, 1
+    )
+    high, low, pos, filled = (found[i * S : (i + 1) * S].astype(I32) for i in range(4))
+    entry = (high * 256 + low) * LANE + pos
+    req_msg[:, 0, :] = jnp.where(filled > 0, entry, -1)
+    start_seq(X_REQ, lambda p: req_msg.at[p], req_all)
+    req_all[me_s] = req_msg[me_s]
 
     wait_seq(X_CONV, rcv1)
     rf[...] = rcv1[...].astype(F32)
@@ -359,9 +355,8 @@
     start_seq(X_BACK, lambda p: msg2.at[p], rcv2)
     rcv2[me_s] = msg2[me_s]
 
-    asked_high = rf[:, 30, :].astype(I32)
-    asked_low = rf[:, 31, :].astype(I32)
-    asked = jnp.where(asked_high < 512, (asked_high + 256) * 512 + asked_low + 256, -1)
+    wait_seq(X_REQ, req_all)
+    asked = req_all[:, 0, :]
     asked = asked.reshape(GROUPS, 2, LANE)
     even_half, odd_half = asked[:, 0, :], asked[:, 1, :]
     first_half = iota((GROUPS, LANE), 1) < NEG
@@ -378,6 +373,16 @@
 
     over(C, me_v, table_along_y)
     tab_all[1, me_v] = tab_own[...]
+    cat_copy.wait()
+
+    def turn(i, carry):
+        span = pl.ds(pl.multiple_of(i * 256, 256), 256)
+        cat_t[0:FULL, span] = cat[span, :].T
+        return carry
+
+    lax.fori_loop(0, ITEMS // 256, turn, 0)
+    cat_t[FULL : FULL + 16, :] = jnp.broadcast_to(cnt[...].astype(F32), (16, ITEMS)).astype(BF16)
+
     row_scale[...] = jnp.zeros_like(row_scale)
     row_log[...] = jnp.zeros_like(row_log)
     item_ids = iota((ITEMS, LANE), 0)
@@ -409,12 +414,31 @@
 
         over(C, mine, fn)
 
+    def chunk_at(i):
+        return jnp.where(i < 2, i, jnp.where(i < EARLY, i + 2, i - 4))
+
+    def send_chunk(h):
+        send_rows(X_ROWS + h, pl.ds(2 * h, 2), pl.ds(2 * h, 2), h < CHUNKS // 2)
+
+    def send_late():
+        send_rows(X_ROWS + CHUNKS, GROUPS, GROUPS, True)
+
+        def step(i, carry):
+            send_chunk(chunk_at(i))
+            return carry
+
+        lax.fori_loop(EARLY, CHUNKS, step, 0)
+
     def fetch(first, last):
         def step(i, carry):
-            h = lax.rem(i, 2) * (CHUNKS // 2) + i // 2
+            h = chunk_at(i)
             hot = jnp.concatenate([picked(2 * h), picked(2 * h + 1)], axis=1)
             keep(dot(cat_t[...], hot), 256, 2 * h)
-            send_rows(X_ROWS + h, pl.ds(2 * h, 2), pl.ds(2 * h, 2), h < CHUNKS // 2)
+
+            @pl.when(i < EARLY)
+            def _():
+                send_chunk(h)
+
             return carry
 
         lax.fori_loop(first, last, step, 0)
@@ -423,7 +447,6 @@
         keep(dot(cat_t[...], picked(GROUPS)), LANE, GROUPS)
         rows_all[GROUPS, me_c] = rows_send[GROUPS, me_c]
         rows_all[GROUPS + 1, me_v] = rows_send[GROUPS, me_v]
-        send_rows(X_ROWS + CHUNKS, GROUPS, GROUPS, True)
         send_rows(X_ROWS + CHUNKS + 1, GROUPS, GROUPS + 1, False)
 
     def each_chunk(fn):
@@ -435,7 +458,7 @@
         for i in range(2):
             fn(X_ROWS + CHUNKS + i, rows_all.at[GROUPS + i, pl.ds(0, C - 1)])
 
-    fetch(0, 4)
+    fetch(0, 5)
     pass_weight(X_WGATE, X_WGATE_MATE, wg_all)
     wait_ch(X_SIG, sig_all)
 
@@ -455,7 +478,7 @@
 
     wait_weight(X_WGATE_MATE, wg_all)
     gate_t[...] = dot(wg_all[...].reshape(FULL, FULL), sig_all[...].reshape(FULL, LANE))
-    fetch(4, 6)
+    fetch(5, 8)
     wait_weight(X_WOUT_MATE, wo_all)
     wo_t[...] = wo_all[...].reshape(FULL, FULL).T
     wait_ch(X_MIX, mix_all)
@@ -463,73 +486,6 @@
     lo_send[...] = dot(wo_t[...], mix.astype(BF16)).astype(BF16).reshape(C, CH, LANE)
     start_ch(X_OUT, lambda p: lo_send.at[p], lo_all)
     lo_all[me_c] = lo_send[me_c]
-
-    fetch(6, 8)
-    tok_pos = spos[...]
-    pos_in = tok_pos >> 2
-    where_in = ((pos_in >> 7) * 4 + (tok_pos & 3)) * LANE + (pos_in & 127)
-    pick = onehot(iota((TOK, LANE), 0) == where_in)
-
-    wait_ch(X_OUT, lo_all)
-    lo_t = jnp.concatenate([lo_all[q] for q in range(8)], axis=1)
-    q_own[...] = dot(lo_t, pick).astype(BF16)
-
-    def along_z(fn):
-        def step(d, carry):
-            fn(lax.rem(me_z + d, layers))
-            return carry
-
-        lax.fori_loop(1, layers, step, 0)
-
-    def go_on(z):
-        block = z * SIDE + me_y
-        first = z < layers // 2
-        src = q_stage.at[z]
-
-        def step(j, carry):
-            y = jnp.where(first, j, me_x)
-            x = jnp.where(first, me_x, j)
-            here = (y == me_y) & (x == me_x)
-
-            @pl.when(jnp.logical_not(here))
-            def _():
-                way = jnp.where(first, X_FORWARD, X_ACROSS)
-                copy_to(way, beside(y, x), src, q_all.at[block]).start()
-
-            @pl.when(here)
-            def _():
-                q_all[block] = q_stage[z]
-
-            return carry
-
-        lax.fori_loop(0, SIDE, step, 0)
-
-    q_stage[me_z] = q_own[...]
-    along_z(
-        lambda z: copy_to(
-            X_QUERY, (z * SIDE + me_y, me_c), q_own, q_stage.at[me_z], X_LAYER + me_z
-        ).start()
-    )
-    go_on(me_z)
-    for q in range(8):
-        out_ref[q % 4, :, (q // 4) * LANE : (q // 4 + 1) * LANE] = lo_all[q]
-
-    def take_layer(z):
-        arrived(X_LAYER + z, q_own)
-        go_on(z)
-
-    along_z(take_layer)
-
-    def each_way(fn):
-        fn(X_FORWARD, q_all.at[pl.ds(0, 12)])
-
-        @pl.when(on_diagonal)
-        def _():
-            fn(X_ACROSS, q_all.at[pl.ds(0, 12)])
-
-        @pl.when(jnp.logical_not(on_diagonal))
-        def _():
-            fn(X_ACROSS, q_all.at[pl.ds(0, 16)])
 
     fetch_targets()
 
@@ -562,18 +518,78 @@
     for g in range(GROUPS + 1):
         slot_pos[g] = onehot(columns[:, g : g + 1] == pos_ids)
 
-    each_chunk(arrived)
-    tgt_rows = []
-    for o, lane0 in enumerate(TGT_LANES):
-        rows = jnp.zeros((CH, LANE), F32)
-        for c in range(C):
-            there = rows_all[GROUPS + o % 2, c].astype(F32)
-            turned = pltpu.roll(there, (16 * c - lane0) % LANE, 1)
-            rows = jnp.where(part_of == c, turned, rows)
-        tgt_rows.append(rows)
+    tok_pos = spos[...]
+    pos_in = tok_pos >> 2
+    where_in = ((pos_in >> 7) * 4 + (tok_pos & 3)) * LANE + (pos_in & 127)
+    pick = onehot(iota((TOK, LANE), 0) == where_in)
+
+    wait_ch(X_OUT, lo_all)
+    lo_t = jnp.concatenate([lo_all[q] for q in range(8)], axis=1)
+    q_own[...] = dot(lo_t, pick).astype(BF16)
+
+    def layer_at(i):
+        near = (i + 1) // 2
+        return lax.rem(me_z + jnp.where(lax.rem(i, 2) == 1, near, layers - near), layers)
+
+    def along_z(fn):
+        def step(i, carry):
+            fn(layer_at(i))
+            return carry
+
+        lax.fori_loop(1, layers, step, 0)
+
+    def go_on(z):
+        block = z * SIDE + me_y
+        first = z < layers // 2
+        src = q_stage.at[z]
+
+        def step(j, carry):
+            y = jnp.where(first, j, me_x)
+            x = jnp.where(first, me_x, j)
+            here = (y == me_y) & (x == me_x)
+
+            @pl.when(jnp.logical_not(here))
+            def _():
+                way = jnp.where(first, X_FORWARD, X_ACROSS)
+                copy_to(way, beside(y, x), src, q_all.at[block], X_WAY + z).start()
+
+            @pl.when(here)
+            def _():
+                q_all[block] = q_stage[z]
+
+            return carry
+
+        lax.fori_loop(0, SIDE, step, 0)
+
+    q_stage[me_z] = q_own[...]
+    along_z(
+        lambda z: copy_to(
+            X_QUERY, (z * SIDE + me_y, me_c), q_own, q_stage.at[me_z], X_LAYER + me_z
+        ).start()
+    )
+    go_on(me_z)
+    send_late()
+    for q in range(8):
+        out_ref[q % 4, :, (q // 4) * LANE : (q // 4 + 1) * LANE] = lo_all[q]
+
+    def take_layer(z):
+        arrived(X_LAYER + z, q_own)
+        go_on(z)
+
+    along_z(take_layer)
+
+    def take_blocks(z):
+        three = (z < layers // 2) | on_diagonal
+
+        @pl.when(three)
+        def _():
+            arrived(X_WAY + z, q_all.at[pl.ds(0, SIDE - 1)])
+
+        @pl.when(jnp.logical_not(three))
+        def _():
+            arrived(X_WAY + z, q_all.at[pl.ds(0, SIDE)])
+
     part[...] = jnp.zeros_like(part)
-
-    each_way(arrived)
 
     def pair(g, carry):
         both = jnp.concatenate([q_all[2 * g], q_all[2 * g + 1]], axis=1)
@@ -587,7 +603,28 @@
             part[g // HALF, c, square_place, :] = jnp.sum(one * one, axis=0, keepdims=True)
         return carry
 
-    lax.fori_loop(0, GROUPS, pair, 0, unroll=2)
+    def take_rows(h, like):
+        arrived(X_ROWS + h, like)
+
+    def layer(i, carry):
+        z = layer_at(i)
+        take_rows(z, rows_all.at[pl.ds(2 * z, 2), pl.ds(0, C - 1)])
+        take_blocks(z)
+        pair(2 * z, 0)
+        pair(2 * z + 1, 0)
+        return carry
+
+    lax.fori_loop(0, layers, layer, 0)
+    for i in range(2):
+        take_rows(CHUNKS + i, rows_all.at[GROUPS + i, pl.ds(0, C - 1)])
+    tgt_rows = []
+    for o, lane0 in enumerate(TGT_LANES):
+        rows = jnp.zeros((CH, LANE), F32)
+        for c in range(C):
+            there = rows_all[GROUPS + o % 2, c].astype(F32)
+            turned = pltpu.roll(there, (16 * c - lane0) % LANE, 1)
+            rows = jnp.where(part_of == c, turned, rows)
+        tgt_rows.append(rows)
     tgt_part = [[[jnp.zeros((1, LANE), F32)] * 2 for _ in range(C)] for _ in range(2)]
     for o, lane0 in enumerate(TGT_LANES):
         wide = jnp.concatenate([q_all[b] for b in TGT_BLOCKS[o]], axis=1)
@@ -633,7 +670,6 @@
     tgt_parts = jnp.concatenate(split_parts(by_block, 3), axis=0)
     targets = dot(tgt_parts, slot_pos[GROUPS])
     targets = targets[0:S] + targets[S : 2 * S] + targets[2 * S : 3 * S]
-    sums[...] = jnp.zeros_like(sums)
     sums[:, 1, :] = targets
     for g in range(GROUPS):
         found = dot(exp_parts, slot_pos[g])
@@ -651,9 +687,19 @@
     loss_ref[...] = jnp.log(jnp.exp(target_logit) + last[0:1]) - target_logit
 
     sent_seq(X_CONV, rcv1)
+    sent_seq(X_REQ, req_all)
     sent_seq(X_BACK, rcv2)
     sent(X_QUERY, q_all.at[pl.ds(0, layers - 1)])
-    each_way(sent)
+    sent(X_FORWARD, q_all.at[pl.ds(0, 12)])
+
+    @pl.when(on_diagonal)
+    def _():
+        sent(X_ACROSS, q_all.at[pl.ds(0, 12)])
+
+    @pl.when(jnp.logical_not(on_diagonal))
+    def _():
+        sent(X_ACROSS, q_all.at[pl.ds(0, 16)])
+
     sent_seq(X_SUMS, sums_all)
     sent_ch(X_SIG, sig_all)
     sent_weight(X_WGATE, X_WGATE_MATE, wg_all)
@@ -707,6 +753,8 @@
         ((CH, LANE), BF16),
         ((S // SIDE, CH, LANE), BF16),
         ((S, CH, LANE), BF16),
+        ((S, 1, LANE), I32),
+        ((S, 1, LANE), I32),
         ((64 * S, LANE), BF16),
         ((64 * S, LANE), F32),
         ((64 * S, LANE), F32),
@@ -725,10 +773,10 @@
         ((GROUPS + 1, LANE, LANE), BF16),
         ((2, C, 32, LANE), F32),
         ((2, C, 32, LANE), F32),
-        ((S, 8, LANE), F32),
-        ((S, 8, LANE), F32),
-        ((8, LANE), F32),
-        ((C, 8, LANE), F32),
+        ((S, 2, LANE), F32),
+        ((S, 2, LANE), F32),
+        ((2, LANE), F32),
+        ((C, 2, LANE), F32),
     ]
     layer_out, loss = pl.pallas_call(
         body,

time: 90.4 us -> 86.2 us (0.954)
  Pallas kernels: 86.9 us -> 82.7 us
    pallas_call x1, Pallas kernels: 86.9 us -> 82.7 us  [per_device(): pl.pallas_call(body, out_shape=(jax.ShapeDtypeStruct((4, CH, 256), BF16),...]
where the time goes in v5:
time: 86.2 us; the launch traced here: 86.1 us
  Pallas kernels  82.7 us (96%)
  local copies, waits for them, and re-layouts  2.75 us (3%)
    pallas_call x1, Pallas kernels, per_device(): pl.pallas_call(body, out_shape=(jax.ShapeDtypeStruct((4, CH, 256), BF16),...  82.7 us
    unnamed x2, local copies, waits for them, and re-layouts  2.75 us

profile of v5, /device:TPU:1, one launch (start us, length us, event | category | flops | bytes accessed | tf_op | source)
XLA Modules:
  0.0 86.1 jit_solution(3394459197176411294)
XLA Ops:
  0.6 82.7 %shard_map.131 = (bf16[4,96,256]{2,1,0:T(8,128)(2,1)}, f32[1,128]{1,0:T(1,128)}) custom-call(bf16[4,96,256]{2,1,0:T(8,128)(2,1)} %bitcast.13, f32[96,256]{1,0:T(8,128)} %bitcast.15, f32[1,96]{1,0:T(1,128)} %bitcast.19, bf16[96,768]{1,0:T(8,128)(2,1)} %bitcast.14, bf16[96,768]{1,0:T(8,128)(2,1)} %w_out.1, bf16[2048,768]{1,0:T(8,128)(2,1)} %cat_hbm.1, ...), custom_call_target="tpu_custom_call" | custom-call | flops 20000000000 | bytes 5000000 | tf_op jit(solution)/shard_map/pallas_call | solution.py:781
  83.3 1.6 %copy.16 = bf16[256,4,96]{0,2,1:T(8,128)(2,1)} copy(bf16[256,4,96]{0,2,1:T(8,128)(2,1)} %bitcast.12) | data formatting | bytes 393216
  85.0 1.1 %copy.17 = f32[128]{0:T(128)} copy(f32[128]{0:T(128)} %bitcast.23) | data formatting | bytes 1024

commit v6 on v5

--- a/solution.py
+++ b/solution.py
@@ -47,7 +47,6 @@
 ) = range(20)
 X_LAYER = X_ROWS + GROUPS // 2 + 2
 CHUNKS = GROUPS // 2
-EARLY = 6
 HALF = GROUPS // 2
 X_WAY = X_LAYER + 8
 EXCHANGES = X_WAY + 8
@@ -178,7 +177,7 @@
             fn(lax.rem(me + d, n))
             return carry
 
-        lax.fori_loop(1, n, step, 0)
+        lax.fori_loop(1, n, step, 0, unroll=n - 1 if n == C else 4)
 
     def start_seq(x, src_of, dst):
         over(S, me_s, lambda p: copy_to(x, (p, me_c), src_of(p), dst.at[me_s]).start())
@@ -415,19 +414,10 @@
         over(C, mine, fn)
 
     def chunk_at(i):
-        return jnp.where(i < 2, i, jnp.where(i < EARLY, i + 2, i - 4))
+        return jnp.where(i == 0, 0, jnp.where(i == 1, 1, jnp.where(i == 2, 4, jnp.where(i == 3, 5, jnp.where(i == 4, 6, jnp.where(i == 5, 7, jnp.where(i == 6, 2, 3)))))))
 
     def send_chunk(h):
         send_rows(X_ROWS + h, pl.ds(2 * h, 2), pl.ds(2 * h, 2), h < CHUNKS // 2)
-
-    def send_late():
-        send_rows(X_ROWS + CHUNKS, GROUPS, GROUPS, True)
-
-        def step(i, carry):
-            send_chunk(chunk_at(i))
-            return carry
-
-        lax.fori_loop(EARLY, CHUNKS, step, 0)
 
     def fetch(first, last):
         def step(i, carry):
@@ -435,7 +425,7 @@
             hot = jnp.concatenate([picked(2 * h), picked(2 * h + 1)], axis=1)
             keep(dot(cat_t[...], hot), 256, 2 * h)
 
-            @pl.when(i < EARLY)
+            @pl.when((h != 1) & (h != 2) & (h != 3))
             def _():
                 send_chunk(h)
 
@@ -447,6 +437,7 @@
         keep(dot(cat_t[...], picked(GROUPS)), LANE, GROUPS)
         rows_all[GROUPS, me_c] = rows_send[GROUPS, me_c]
         rows_all[GROUPS + 1, me_v] = rows_send[GROUPS, me_v]
+        send_rows(X_ROWS + CHUNKS, GROUPS, GROUPS, True)
         send_rows(X_ROWS + CHUNKS + 1, GROUPS, GROUPS + 1, False)
 
     def each_chunk(fn):
@@ -474,6 +465,7 @@
         mix_send[q] = (conv + gain_col * sig_send[q].astype(F32)).astype(BF16)
     start_ch(X_MIX, lambda p: mix_send.at[p], mix_all)
     mix_all[me_c] = mix_send[me_c]
+    send_chunk(1)
     pass_weight(X_WOUT, X_WOUT_MATE, wo_all)
 
     wait_weight(X_WGATE_MATE, wg_all)
@@ -486,6 +478,8 @@
     lo_send[...] = dot(wo_t[...], mix.astype(BF16)).astype(BF16).reshape(C, CH, LANE)
     start_ch(X_OUT, lambda p: lo_send.at[p], lo_all)
     lo_all[me_c] = lo_send[me_c]
+    send_chunk(2)
+    send_chunk(3)
 
     fetch_targets()
 
@@ -568,7 +562,6 @@
         ).start()
     )
     go_on(me_z)
-    send_late()
     for q in range(8):
         out_ref[q % 4, :, (q // 4) * LANE : (q // 4 + 1) * LANE] = lo_all[q]
 

time: 86.2 us -> 81.1 us (0.941)
  Pallas kernels: 82.7 us -> 77.5 us
    pallas_call x1, Pallas kernels: 82.7 us -> 77.5 us  [per_device(): pl.pallas_call(body, out_shape=(jax.ShapeDtypeStruct((4, CH, 256), BF16),...]
where the time goes in v6:
time: 81.1 us; the launch traced here: 80.9 us
  Pallas kernels  77.5 us (96%)
  local copies, waits for them, and re-layouts  2.75 us (3%)
    pallas_call x1, Pallas kernels, per_device(): pl.pallas_call(body, out_shape=(jax.ShapeDtypeStruct((4, CH, 256), BF16),...  77.5 us
    unnamed x2, local copies, waits for them, and re-layouts  2.75 us

profile of v6, /device:TPU:1, one launch (start us, length us, event | category | flops | bytes accessed | tf_op | source)
XLA Modules:
  0.0 80.9 jit_solution(3316401007973045721)
XLA Ops:
  0.6 77.5 %shard_map.131 = (bf16[4,96,256]{2,1,0:T(8,128)(2,1)}, f32[1,128]{1,0:T(1,128)}) custom-call(bf16[4,96,256]{2,1,0:T(8,128)(2,1)} %bitcast.13, f32[96,256]{1,0:T(8,128)} %bitcast.15, f32[1,96]{1,0:T(1,128)} %bitcast.19, bf16[96,768]{1,0:T(8,128)(2,1)} %bitcast.14, bf16[96,768]{1,0:T(8,128)(2,1)} %w_out.1, bf16[2048,768]{1,0:T(8,128)(2,1)} %cat_hbm.1, ...), custom_call_target="tpu_custom_call" | custom-call | flops 20000000000 | bytes 5000000 | tf_op jit(solution)/shard_map/pallas_call | solution.py:774
  78.2 1.6 %copy.16 = bf16[256,4,96]{0,2,1:T(8,128)(2,1)} copy(bf16[256,4,96]{0,2,1:T(8,128)(2,1)} %bitcast.12) | data formatting | bytes 393216
  79.8 1.1 %copy.17 = f32[128]{0:T(128)} copy(f32[128]{0:T(128)} %bitcast.23) | data formatting | bytes 1024

commit v7 on v6

--- a/solution.py
+++ b/solution.py
@@ -77,21 +77,32 @@
 
 
 def body(
+    sig_hbm,
+    taps_t_hbm,
+    gain_hbm,
+    wg_own_hbm,
+    w_out_hbm,
+    cat_hbm,
+    cnt_hbm,
+    spos_hbm,
+    nown_hbm,
+    nrow_hbm,
+    town_hbm,
+    trow_hbm,
+    out_ref,
+    loss_ref,
     sig,
     taps_t,
     gain,
     wg_own,
     w_out,
-    cat_hbm,
+    cat,
     cnt,
     spos,
     nown,
     nrow,
     town,
     trow,
-    out_ref,
-    loss_ref,
-    cat,
     sig_send,
     sig_all,
     msgf,
@@ -140,7 +151,7 @@
     fin_all,
     send_sem,
     recv_sem,
-    cat_sem,
+    load_sem,
 ):
     me_s = lax.axis_index("seq")
     me_c = lax.axis_index("ch")
@@ -220,8 +231,16 @@
 
     on_diagonal = me_x == me_y
 
-    cat_copy = pltpu.make_async_copy(cat_hbm, cat, cat_sem)
-    cat_copy.start()
+    far = (sig_hbm, taps_t_hbm, gain_hbm, wg_own_hbm, w_out_hbm, cat_hbm, cnt_hbm, spos_hbm, nown_hbm, nrow_hbm, town_hbm, trow_hbm)
+    near = (sig, taps_t, gain, wg_own, w_out, cat, cnt, spos, nown, nrow, town, trow)
+    loads = [
+        pltpu.make_async_copy(src, dst, load_sem.at[i])
+        for i, (src, dst) in enumerate(zip(far, near))
+    ]
+    for load in loads:
+        load.start()
+    for i in (0, 1):
+        loads[i].wait()
 
     for q in range(8):
         piece = sig[q % 4, :, (q // 4) * LANE : (q // 4 + 1) * LANE]
@@ -240,6 +259,8 @@
     extra = SIDE - 1 + SIDE - jnp.where(on_diagonal, 1, 0)
     pl.semaphore_wait(barrier, S - 1 + C - 1 + extra)
 
+    for i in (2, 3, 4, 6, 7, 8, 9, 10, 11):
+        loads[i].wait()
     start_seq(X_CONV, lambda p: msg1.at[p], rcv1)
     rcv1[me_s] = msg1[me_s]
     start_ch(X_SIG, lambda p: sig_send.at[p], sig_all)
@@ -372,7 +393,7 @@
 
     over(C, me_v, table_along_y)
     tab_all[1, me_v] = tab_own[...]
-    cat_copy.wait()
+    loads[5].wait()
 
     def turn(i, carry):
         span = pl.ds(pl.multiple_of(i * 256, 256), 256)
@@ -723,7 +744,18 @@
 ):
     vmem = pl.BlockSpec(memory_space=pltpu.VMEM)
     scratch = [
+        ((4, CH, 256), BF16),
+        ((CH, 256), F32),
+        ((1, CH), F32),
+        ((CH, FULL), BF16),
+        ((CH, FULL), BF16),
         ((ITEMS, FULL), BF16),
+        ((1, ITEMS), I32),
+        ((1, LANE), I32),
+        ((64, 1, LANE), I32),
+        ((64, LANE), I32),
+        ((1, LANE), I32),
+        ((1, LANE), I32),
         ((C, CH, LANE), BF16),
         ((C, CH, LANE), BF16),
         ((S * 32, LANE), F32),
@@ -777,11 +809,11 @@
             jax.ShapeDtypeStruct((4, CH, 256), BF16),
             jax.ShapeDtypeStruct((1, LANE), F32),
         ),
-        in_specs=[vmem] * 5 + [pl.BlockSpec(memory_space=pl.ANY)] + [vmem] * 6,
+        in_specs=[pl.BlockSpec(memory_space=pl.ANY)] * 12,
         out_specs=(vmem, vmem),
         scratch_shapes=[pltpu.VMEM(shape, kind) for shape, kind in scratch]
         + [pltpu.SemaphoreType.DMA((EXCHANGES,))] * 2
-        + [pltpu.SemaphoreType.DMA(())],
+        + [pltpu.SemaphoreType.DMA((12,))],
         compiler_params=pltpu.CompilerParams(
             collective_id=0, has_side_effects=True, vmem_limit_bytes=60 * 1024 * 1024
         ),

time: 81.1 us -> 80.3 us (level)
  no operation moved by 1% of the time
where the time goes in v7:
time: 80.3 us; the launch traced here: 80.2 us
  Pallas kernels  76.8 us (96%)
  local copies, waits for them, and re-layouts  2.75 us (3%)
    pallas_call x1, Pallas kernels, per_device(): pl.pallas_call(body, out_shape=(jax.ShapeDtypeStruct((4, CH, 256), BF16),...  76.8 us
    unnamed x2, local copies, waits for them, and re-layouts  2.75 us

profile of v7, /device:TPU:1, one launch (start us, length us, event | category | flops | bytes accessed | tf_op | source)
XLA Modules:
  0.0 80.2 jit_solution(17612623006876109721)
XLA Ops:
  0.6 76.8 %shard_map.131 = (bf16[4,96,256]{2,1,0:T(8,128)(2,1)}, f32[1,128]{1,0:T(1,128)}) custom-call(bf16[4,96,256]{2,1,0:T(8,128)(2,1)} %bitcast.13, f32[96,256]{1,0:T(8,128)} %bitcast.15, f32[1,96]{1,0:T(1,128)} %bitcast.19, bf16[96,768]{1,0:T(8,128)(2,1)} %bitcast.14, bf16[96,768]{1,0:T(8,128)(2,1)} %w_out_hbm.1, bf16[2048,768]{1,0:T(8,128)(2,1)} %cat_hbm.1, ...), custom_call_target="tpu_custom_call" | custom-call | flops 20000000000 | bytes 5000000 | tf_op jit(solution)/shard_map/pallas_call | solution.py:806
  77.4 1.6 %copy.16 = bf16[256,4,96]{0,2,1:T(8,128)(2,1)} copy(bf16[256,4,96]{0,2,1:T(8,128)(2,1)} %bitcast.12) | data formatting | bytes 393216
  79.0 1.1 %copy.17 = f32[128]{0:T(128)} copy(f32[128]{0:T(128)} %bitcast.23) | data formatting | bytes 1024
